TPU v7x, 32 devices: a whole 2x2x4 slice. The times are simulated.
32 devices in a mesh: chan: 16 (over z, y, core), stn: 2 (over x).
Axes of the slice: x: 2, y: 2, z: 4, core: 2. Of those that a mesh axis runs over, the one named last changes fastest.
Arguments:
- voltages: bfloat16 [1024, 196608], P('stn', 'chan'), may hold values from -6 to 6
- pfb_taps: float32 [16, 512], replicated, may hold values from -1.5 to 1.5
- flags: int32 [512, 256, 48], P('stn', 'chan'), may hold values 0 or 1
Outputs:
- visibilities: float32 [256, 2, 1024, 1024], P('chan', None, 'stn')
All inputs are finite; a program needn't handle non-finite values. No bound on the sum of `flags` on one device may be relied on, other than what follows from the above.
Results may differ from a plain program's by a relative error of at most 0.0062.
Values may be sent and summed in bfloat16 or wider, within the bound.
No kernel may reach another device: no remote copies, remote signals or barrier semaphores. Data moves between devices by JAX's collectives and lax.ppermute only.
A program may use at most 320 MiB of HBM per device.

v0:
```python
import math

import jax
import jax.numpy as jnp
from jax import lax
from jax.sharding import PartitionSpec as P

POLS = 2


def shifted(block, axis, distance):
    devices = range(lax.axis_size(axis))
    route = [(i - distance, i) for i in devices if i - distance in devices]
    return lax.ppermute(block, axis, route)


def dft_table(length):
    rows_index = jnp.arange(length, dtype=jnp.int32)
    chan_index = rows_index // 2
    sample_index = jnp.arange(length, dtype=jnp.int32)
    phase_step = chan_index[:, None] * sample_index[None, :] % length
    angles = phase_step.astype(jnp.float32) * (2.0 * math.pi / length)
    values = jnp.where((rows_index % 2 == 0)[:, None], jnp.cos(angles), -jnp.sin(angles))
    return (values / math.sqrt(length)).astype(jnp.bfloat16)


def cross_tile(local, remote, count):
    prods = jnp.einsum("cpat,cqbt->cpqab", local, remote, preferred_element_type=jnp.float32)
    real_part = prods[:, 0, 0] + prods[:, 1, 1]
    imag_part = prods[:, 1, 0] - prods[:, 0, 1]
    return jnp.stack([real_part, imag_part], axis=1) / count


def shards(voltages, pfb_taps, flags):
    taps = pfb_taps.shape[0]
    length = pfb_taps.shape[1]
    local_signals = voltages.shape[0]
    spec_local = voltages.shape[1] // length
    frames = voltages.reshape(local_signals, spec_local, length)
    earlier = shifted(frames[:, spec_local - (taps - 1) :, :], "chan", 1)
    padded = jnp.concatenate([earlier, frames], axis=1)
    filtered = jnp.zeros((local_signals, spec_local, length), jnp.float32)
    for tap_index in range(taps):
        offset = taps - 1 - tap_index
        filtered = filtered + pfb_taps[tap_index] * padded[:, offset : offset + spec_local, :]
    filtered = filtered.astype(jnp.bfloat16)
    spectra = jnp.einsum(
        "qn,stn->qst", dft_table(length), filtered, preferred_element_type=jnp.float32
    ).astype(jnp.bfloat16)
    turned = lax.all_to_all(spectra, "chan", split_axis=0, concat_axis=2, tiled=True)
    chan_local = turned.shape[0] // 2
    total = turned.shape[2]
    stations_local = flags.shape[0]
    blocks = flags.shape[2]
    keep = jnp.transpose(flags, (1, 0, 2)).astype(jnp.bfloat16)[:, None, :, None, :, None]
    shaped = turned.reshape(chan_local, 2, stations_local, POLS, blocks, total // blocks)
    weighted = (shaped * keep).reshape(chan_local, 2, local_signals, total)
    count = float(total)
    return cross_tile(weighted, lax.all_gather(weighted, "stn", axis=2, tiled=True), count)


def solution(mesh):
    placed = (P("stn", "chan"), P(), P("stn", "chan", None))
    return jax.shard_map(
        shards, mesh=mesh, in_specs=placed, out_specs=P("chan", None, "stn", None), check_vma=False
    )
```

profile of v0, /device:TPU:0, one launch (start us, length us, event | category | flops | bytes accessed | tf_op | source)
XLA Modules:
  0.0 1083.3 jit_solution(17672340423868391474)
XLA Ops:
  6.5 10.6 copy.57
  17.2 3.7 slice.144
  20.9 5.4 collective-permute-start
  26.4 5.1 fusion.37
  31.4 4.0 collective-permute-done
  35.4 7.2 constant_dynamic-update-slice_fusion.1
  42.6 10.6 constant_dynamic-update-slice_fusion
  53.2 84.3 %fusion.6 = bf16[512,512,24]{1,0,2:T(8,128)(2,1)} fusion(bf16[512,39,512]{2,0,1:T(8,128)(2,1)} %constant_dynamic-update-slice_fusion, f32[512]{0:T(512)S(1)} %bitcast.89, f32[512]{0:T(512)S(1)} %bitcast.90, f32[512]{0:T(512)S(1)} %bitcast.76, f32[512]{0:T(512)S(1)} %bitcast.77, f32[512]{0:T(512)S(1)} %bitcast.78, f32[512]{0:T(512)S(1)} %bitcast.79, ...), kind=kOutput, calls=%fused_computation.13 | convolution fusion | flops 6750732288 | bytes 214466560 | tf_op jit(solution)/shard_map/qn,stn->qst/dot_general | solution.py:47
  137.5 14.6 %copy.35 = bf16[512,512,24]{1,2,0:T(8,128)(2,1)} copy(bf16[512,512,24]{1,0,2:T(8,128)(2,1)} %fusion.6) | data formatting | bytes 25165824 | tf_op jit(solution)/shard_map/convert_element_type | solution.py:49
  152.1 82.2 %all-to-all-start = ((bf16[512,512,24]{1,2,0:T(8,128)(2,1)}), bf16[512,512,24]{1,2,0:T(8,128)(2,1)}, u32[]{:S(2)}, u32[]{:S(2)}) async-start(bf16[512,512,24]{1,2,0:T(8,128)(2,1)} %copy.35), calls=%async_computation | async-start | bytes 25165824 | tf_op jit(solution)/shard_map/all_to_all | solution.py:50
  234.2 0.2 all-gather.2.cloned.1.call-start
  234.6 3.1 copy.37
  237.6 16.6 %mul.245 = bf16[16,256,2,48,8]{0,4,3,2,1:T(8,128)(2,1)} broadcast(bf16[16,256,48]{0,2,1:T(8,128)(2,1)S(1)} %copy.37), dimensions={0,1,3} | broadcast | bytes 6684672 | tf_op jit(solution)/shard_map/mul | solution.py:57
  254.2 38.0 %copy.38 = bf16[16,512,384]{2,1,0:T(8,128)(2,1)} copy(bf16[16,512,384]{0,2,1:T(8,128)(2,1)} %bitcast.69) | data formatting | bytes 12582912 | tf_op jit(solution)/shard_map/mul | solution.py:57
  292.2 165.8 %all-to-all-done = bf16[512,512,24]{1,2,0:T(8,128)(2,1)} async-done(((bf16[512,512,24]{1,2,0:T(8,128)(2,1)}), bf16[512,512,24]{1,2,0:T(8,128)(2,1)}, u32[]{:S(2)}, u32[]{:S(2)}) %all-to-all-start) | async-done | bytes 12582944 | tf_op jit(solution)/shard_map/all_to_all | solution.py:50
  458.0 10.8 copy.36
  468.8 16.6 %copy.39 = bf16[16,2,512,384]{3,2,1,0:T(8,128)(2,1)} copy(bf16[16,2,512,384]{2,3,1,0:T(8,128)(2,1)} %bitcast.73) | data formatting | bytes 25165824 | tf_op jit(solution)/shard_map/reshape | solution.py:56
  485.4 11.6 %broadcast_multiply_fusion = bf16[16,2,512,384]{3,2,1,0:T(8,128)(2,1)} fusion(bf16[16,2,512,384]{3,2,1,0:T(8,128)(2,1)} %copy.39, bf16[16,512,384]{2,1,0:T(8,128)(2,1)} %copy.38), kind=kLoop, calls=%fused_computation.14 | loop fusion | flops 6291456 | bytes 31457280 | tf_op jit(solution)/shard_map/mul | solution.py:57
  497.0 344.3 %all-gather.2.cloned.1.call-done = bf16[16,2,1024,384]{3,2,1,0:T(8,128)(2,1)} async-done(((bf16[16,2,512,384]{3,2,1,0:T(8,128)(2,1)}), bf16[16,2,1024,384]{3,2,1,0:T(8,128)(2,1)}) %all-gather.2.cloned.1.call-update) | async-done | bytes 25165840 | tf_op jit(solution)/shard_map/all_gather | solution.py:59
  841.3 61.4 %convolution_bitcast_fusion = f32[16,2,2,512,1024]{3,4,1,2,0:T(8,128)} fusion(bf16[16,2,1024,384]{3,2,1,0:T(8,128)(2,1)} %all-gather.2.cloned.1.call-done, bf16[16,2,512,384]{3,2,1,0:T(8,128)(2,1)} %broadcast_multiply_fusion), kind=kOutput, calls=%fused_computation.1 | convolution fusion | flops 25769803776 | bytes 171966464 | tf_op jit(solution)/shard_map/cpat,cqbt->cpqab/dot_general | solution.py:28
  902.7 33.2 %fusion = f32[16,1,512,1024]{2,3,0,1:T(8,128)} fusion(f32[16,2,2,512,1024]{3,4,1,2,0:T(8,128)} %convolution_bitcast_fusion), kind=kLoop, calls=%fused_computation.3 | loop fusion | flops 8388608 | bytes 100663296 | tf_op jit(solution)/shard_map/sub | solution.py:30
  935.9 33.1 %fusion.2 = f32[16,1,512,1024]{2,3,0,1:T(8,128)} fusion(f32[16,2,2,512,1024]{3,4,1,2,0:T(8,128)} %convolution_bitcast_fusion), kind=kLoop, calls=%fused_computation.6 | loop fusion | flops 8388608 | bytes 100663296 | tf_op jit(solution)/shard_map/add | solution.py:29
  969.0 44.8 %maximum_multiply_fusion = f32[16,2,512,1024]{2,3,0,1:T(8,128)} fusion(f32[16,1,512,1024]{2,3,0,1:T(8,128)} %fusion, f32[16,1,512,1024]{2,3,0,1:T(8,128)} %fusion.2), kind=kLoop, calls=%fused_computation | loop fusion | flops 33554432 | bytes 134217728 | tf_op jit(solution)/shard_map/div | solution.py:31
  1013.8 62.6 %copy.42 = f32[16,2,512,1024]{3,2,1,0:T(8,128)} copy(f32[16,2,512,1024]{2,3,0,1:T(8,128)} %maximum_multiply_fusion) | data formatting | bytes 134217728 | tf_op jit(solution)/shard_map/div | solution.py:31
  (9 shorter events, 0.1 us)
Async XLA Ops:
  6.5 19.8 %copy-start.1 = (f32[16,512]{1,0:T(8,128)S(1)}, f32[16,512]{1,0:T(8,128)}, u32[]{:S(2)}) copy-start(f32[16,512]{1,0:T(8,128)} %param.4) | copy-start | bytes 98308
  20.9 14.5 %collective-permute-start = (bf16[512,15,512]{2,0,1:T(8,128)(2,1)S(1)}, bf16[512,15,512]{2,0,1:T(8,128)(2,1)}, u32[]{:S(2)}, u32[]{:S(2)}) collective-permute-start(bf16[512,15,512]{2,0,1:T(8,128)(2,1)S(1)} %slice.144), channel_id=1, source_target_pairs={{0,2},{2,4},{4,6},{6,8},{8,10},{10,12},{12,14},{14,16},{16,18},{18... | collective-permute-start | bytes 23592968 | tf_op jit(solution)/shard_map/ppermute | solution.py:14
  137.5 97.0 %copy-start = (s32[256,16,48]{0,2,1:T(8,128)S(1)}, s32[256,16,48]{0,2,1:T(8,128)}, u32[]{:S(2)}) copy-start(s32[256,16,48]{0,2,1:T(8,128)} %param.5) | copy-start | bytes 2359300
  152.1 305.9 %all-to-all-start = ((bf16[512,512,24]{1,2,0:T(8,128)(2,1)}), bf16[512,512,24]{1,2,0:T(8,128)(2,1)}, u32[]{:S(2)}, u32[]{:S(2)}) async-start(bf16[512,512,24]{1,2,0:T(8,128)(2,1)} %copy.35), calls=%async_computation | async-start | bytes 25165824 | tf_op jit(solution)/shard_map/all_to_all | solution.py:50
  234.2 607.1 %all-gather.2.cloned.1.call-start = ((), (), s32[]{:S(2)}) async-start(), calls=%async_computation.1 | async-start | bytes 37748736 | tf_op jit(solution)/shard_map/all_gather | solution.py:59
Sparse Core Ops, SparseCore 0:
  497.1 344.1 all-gather.1
where the time goes:
time: 1090 us; the launch traced here: 1080 us
  waiting for transfers between devices  514 us (47%)
  local copies, waits for them, and re-layouts  194 us (18%)
  matrix products  146 us (13%)
  other arithmetic  128 us (12%)
  starting transfers between devices  87.8 us (8%)
  between operations  13.5 us (1%)
    all_gather x1, waiting for transfers between devices, shards(): lax.all_gather(weighted, 'stn', axis=2, tiled=True)  344 us
    all_to_all x1, waiting for transfers between devices, shards(): lax.all_to_all(spectra, 'chan', split_axis=0, concat_axis=2, tiled=True)  166 us
    dot_general x1, matrix products, shards(): jnp.einsum('qn,stn->qst', dft_table(length), filtered, preferred_element_...  84.3 us
    all_to_all x1, starting transfers between devices, shards(): lax.all_to_all(spectra, 'chan', split_axis=0, concat_axis=2, tiled=True)  82.2 us
    div x1, local copies, waits for them, and re-layouts, cross_tile(): return jnp.stack([real_part, imag_part], axis=1) / count  62.6 us
    dot_general x1, matrix products, cross_tile(): jnp.einsum('cpat,cqbt->cpqab', local, remote, preferred_element_type=jnp....  61.4 us
    mul x2, local copies, waits for them, and re-layouts, shards(): weighted = (shaped * keep).reshape(chan_local, 2, local_signals, total)  54.5 us
    div x1, other arithmetic, cross_tile(): return jnp.stack([real_part, imag_part], axis=1) / count  44.8 us
  transfers between devices with their start and end apart: 3, of which 3 were waited for; matrix products, arithmetic and copies ran while one was open for 6% of the time, Pallas kernels for 0%

commit v1 on v0

v1 whole, which is shorter than its diff:
```python
import functools
import math

import jax
import jax.numpy as jnp
import numpy as np
from jax import lax
from jax.experimental import pallas as pl
from jax.experimental.pallas import tpu as pltpu
from jax.sharding import PartitionSpec as P

POLS = 2
LANES = 128
ROWS = 16
STEP = 8
VMEM = 56 * 1024 * 1024
BF16 = jnp.bfloat16
F32 = jnp.float32


def shifted(block, axis, distance):
    devices = range(lax.axis_size(axis))
    route = [(i - distance, i) for i in devices if i - distance in devices]
    return lax.ppermute(block, axis, route)


def swapped(block, axis, mask):
    return lax.ppermute(block, axis, [(i, i ^ mask) for i in range(lax.axis_size(axis))])


def dft_table(length):
    rows_index = np.arange(length)
    phase = (rows_index // 2)[:, None] * np.arange(length)[None, :] % length
    angles = phase.astype(np.float32) * np.float32(2.0 * math.pi / length)
    values = np.where((rows_index % 2 == 0)[:, None], np.cos(angles), -np.sin(angles))
    return (values / np.float32(math.sqrt(length))).astype(np.float32)


def spectra_kernel(start, count, has_halo, *refs):
    if has_halo:
        halo_ref, refs = refs[0], refs[1:]
    volts_ref, taps_ref, table_ref = refs[:3]
    outs, (filt_ref, res_ref) = refs[3:-2], refs[-2:]
    taps, length = taps_ref.shape
    signals = volts_ref.shape[0]

    def frame(rows, j, n0):
        if j < 0:
            return halo_ref[rows, pl.ds((j + taps - 1) * length + n0, LANES)].astype(F32)
        return volts_ref[rows, pl.ds(j * length + n0, LANES)].astype(F32)

    def body(g, carry):
        rows = pl.ds(pl.multiple_of(g * ROWS, ROWS), ROWS)
        for n0 in range(0, length, LANES):
            coef = [taps_ref[k : k + 1, n0 : n0 + LANES] for k in range(taps)]
            for t0 in range(0, count, STEP):
                sums = [None] * STEP
                for j in range(start + t0 - (taps - 1), start + t0 + STEP):
                    value = frame(rows, j, n0)
                    for t in range(STEP):
                        k = start + t0 + t - j
                        if 0 <= k < taps:
                            term = coef[k] * value
                            sums[t] = term if sums[t] is None else sums[t] + term
                for t in range(STEP):
                    filt_ref[t0 + t, rows, n0 : n0 + LANES] = sums[t].astype(BF16)
        return carry

    lax.fori_loop(0, signals // ROWS, body, 0)
    for t in range(count):
        res_ref[pl.ds(t, length, stride=count), :] = lax.dot_general(
            table_ref[...], filt_ref[t], (((1,), (1,)), ((), ())), preferred_element_type=F32
        )
    rows = length * count // len(outs)
    for i, out in enumerate(outs):
        out[...] = res_ref[i * rows : (i + 1) * rows, :].astype(BF16)


def spectra(volts, halo, taps, table, start, count, pieces):
    signals = volts.shape[0]
    length = taps.shape[1]
    block = min(LANES, signals)
    width = (start + count) * length
    rows = length * count // pieces
    in_specs = [
        pl.BlockSpec((block, width), lambda s: (s, 0)),
        pl.BlockSpec(taps.shape, lambda s: (0, 0)),
        pl.BlockSpec(table.shape, lambda s: (0, 0)),
    ]
    args = (volts, taps, table)
    if halo is not None:
        in_specs.insert(0, pl.BlockSpec((block, halo.shape[1]), lambda s: (s, 0)))
        args = (halo,) + args
    return pl.pallas_call(
        functools.partial(spectra_kernel, start, count, halo is not None),
        grid=(signals // block,),
        in_specs=in_specs,
        out_specs=[pl.BlockSpec((rows, block), lambda s: (0, s))] * pieces,
        out_shape=[jax.ShapeDtypeStruct((rows, signals), BF16)] * pieces,
        scratch_shapes=[
            pltpu.VMEM((count, block, length), BF16),
            pltpu.VMEM((length * count, block), F32),
        ],
        compiler_params=pltpu.CompilerParams(vmem_limit_bytes=VMEM),
        cost_estimate=pl.CostEstimate(
            flops=2 * length * length * count * signals * 5,
            bytes_accessed=2 * signals * (width + length * count),
            transcendentals=0,
        ),
    )(*args)


def join_kernel(count, *refs):
    pieces, keep_ref, out_ref = refs[:-2], refs[-2], refs[-1]
    blocks = count // STEP
    for c in range(out_ref.shape[0]):
        parts = [[], []]
        for p, piece in enumerate(pieces):
            values = piece[c * 2 * count : (c + 1) * 2 * count, :].astype(F32)
            for r in range(2):
                for b in range(blocks):
                    at = r * count + b * STEP
                    i = p * blocks + b
                    parts[r].append(values[at : at + STEP] * keep_ref[c, i : i + 1, :])
        for r in range(2):
            out_ref[c, r] = jnp.concatenate(parts[r], axis=0).astype(BF16)


def joined(pieces, keep, count):
    chans = keep.shape[0]
    signals = keep.shape[2]
    frames = len(pieces) * count
    group = math.gcd(chans, 4)
    return pl.pallas_call(
        functools.partial(join_kernel, count),
        grid=(chans // group,),
        in_specs=[pl.BlockSpec((group * 2 * count, signals), lambda c: (c, 0))] * len(pieces)
        + [pl.BlockSpec((group,) + keep.shape[1:], lambda c: (c, 0, 0))],
        out_specs=pl.BlockSpec((group, 2, frames, signals), lambda c: (c, 0, 0, 0)),
        out_shape=jax.ShapeDtypeStruct((chans, 2, frames, signals), BF16),
        compiler_params=pltpu.CompilerParams(vmem_limit_bytes=VMEM),
        cost_estimate=pl.CostEstimate(
            flops=chans * 2 * frames * signals,
            bytes_accessed=8 * chans * frames * signals,
            transcendentals=0,
        ),
    )(*pieces, keep)


def correlate_kernel(parts, widths, scale, place_ref, *refs):
    out_ref, (lhs_re, lhs_im, rhs) = refs[-4], refs[-3:]
    groups = len(parts)
    total = sum(parts)
    for side in range(len(widths)):
        mine = refs[side * groups : (side + 1) * groups]
        for r in range(2):
            at = r * total
            for ref, rows in zip(mine, parts):
                rhs[at : at + rows, : widths[side]] = ref[0, r]
                at += rows
        if side == 0:
            turned = rhs[:, : widths[0]].T
            lhs_re[...] = turned
            lhs_im[:, :total] = turned[:, total:]
            lhs_im[:, total:] = -turned[:, :total]
            if widths[0] != out_ref.shape[3] // len(widths):
                continue
        columns = pl.ds(pl.multiple_of(place_ref[side] * LANES, LANES), widths[side])
        for r, lhs in enumerate((lhs_re, lhs_im)):
            out_ref[0, r, :, columns] = scale * jnp.dot(
                lhs[...], rhs[:, : widths[side]], preferred_element_type=F32
            )


def correlated(result, first, chans, local, others, place, shape, scale):
    operands = local + others
    parts = [array.shape[2] for array, _ in local]
    widths = [group[0][0].shape[3] for group in (local, others)]
    signals = widths[0]
    in_specs = [
        pl.BlockSpec((1, 2) + array.shape[2:], functools.partial(lambda b, c, place: (c + b, 0, 0, 0), first - begin))
        for array, begin in operands
    ]
    args = [array for array, _ in operands]
    aliases = {}
    if result is not None:
        in_specs.append(pl.BlockSpec(memory_space=pl.ANY))
        aliases = {1 + len(args): 0}
        args.append(result)
    total = sum(parts)
    return pl.pallas_call(
        functools.partial(correlate_kernel, parts, widths, scale),
        grid_spec=pltpu.PrefetchScalarGridSpec(
            num_scalar_prefetch=1,
            grid=(chans,),
            in_specs=in_specs,
            out_specs=pl.BlockSpec((1,) + shape[1:], lambda c, place: (c + first, 0, 0, 0)),
            scratch_shapes=[
                pltpu.VMEM((signals, 2 * total), BF16),
                pltpu.VMEM((signals, 2 * total), BF16),
                pltpu.VMEM((2 * total, max(widths)), BF16),
            ],
        ),
        out_shape=jax.ShapeDtypeStruct(shape, F32),
        input_output_aliases=aliases,
        compiler_params=pltpu.CompilerParams(vmem_limit_bytes=VMEM),
        cost_estimate=pl.CostEstimate(
            flops=8 * chans * total * signals * shape[3],
            bytes_accessed=4 * chans * 2 * signals * shape[3],
            transcendentals=0,
        ),
    )(place, *args)


GROUP = 4
SPLITS = 2


def shards(voltages, pfb_taps, flags):
    taps, length = pfb_taps.shape
    signals = voltages.shape[0]
    frames = voltages.shape[1] // length
    devices = lax.axis_size("chan")
    me = lax.axis_index("chan")
    stns = lax.axis_size("stn")
    chans = length // 2 // devices
    total = frames * devices
    blocks = flags.shape[2] // devices
    early, late = taps, frames - taps

    halo = shifted(voltages[:, (frames - taps + 1) * length :], "chan", 1)

    order = jnp.arange(devices, dtype=jnp.int32) ^ me
    table = jnp.take(jnp.asarray(dft_table(length)).astype(BF16).reshape(devices, -1, length), order, axis=0)
    late_table = table.reshape(length, length)
    early_table = table.reshape(devices, SPLITS, -1, length).transpose(1, 0, 2, 3).reshape(length, length)

    sent_late = spectra(voltages, None, pfb_taps, late_table, early, late, devices)
    sent_early = spectra(voltages, halo, pfb_taps, early_table, 0, early, devices * SPLITS)

    flags, _ = lax.optimization_barrier((flags, sent_late[0]))
    keep = jnp.repeat(jnp.transpose(flags, (1, 2, 0)).astype(F32), POLS, axis=2)
    keep = jnp.take(keep.reshape(chans, devices, blocks, signals), order, axis=1)
    early_blocks = early * blocks // frames

    def exchanged(block):
        if stns == 2:
            return swapped(block, "stn", 1)
        return lax.all_gather(block, "stn", axis=3, tiled=True)

    def moved(sent, keep, count, begin):
        local, others = [], []
        for g in range(0, devices, GROUP):
            got = [swapped(sent[r], "chan", r) if r else sent[r] for r in range(g, g + GROUP)]
            held = keep[:, g : g + GROUP].reshape(keep.shape[0], -1, signals)
            block = joined(got, held, count)
            local.append((block, begin))
            others.append((exchanged(block), begin))
        return local, others

    local_late, others_late = moved(sent_late, keep[:, :, early_blocks:], late, 0)
    if stns == 2:
        place = lax.axis_index("stn") ^ jnp.arange(2, dtype=jnp.int32)
    else:
        place = jnp.zeros((2,), jnp.int32)
    place = place * (signals // LANES)
    result = None
    part = chans // SPLITS
    for k in range(SPLITS):
        begin = k * part
        local, others = moved(
            sent_early[k * devices : (k + 1) * devices], keep[begin : begin + part, :, :early_blocks], early, begin
        )
        result = correlated(
            result, begin, part, local_late + local, others_late + others, place,
            (chans, 2, signals, signals * stns), 1.0 / total,
        )
    return result


def solution(mesh):
    placed = (P("stn", "chan"), P(), P("stn", "chan", None))
    return jax.shard_map(
        shards, mesh=mesh, in_specs=placed, out_specs=P("chan", None, "stn", None), check_vma=False
    )
```

time: 1090 us -> 704 us (0.65)
  waiting for transfers between devices: 514 us -> 317 us
  local copies, waits for them, and re-layouts: 194 us -> 43.6 us
  matrix products: 146 us -> 0 us
  Pallas kernels: 0 us -> 128 us
  other arithmetic: 128 us -> 2.62 us
  starting transfers between devices: 87.8 us -> 201 us
  between operations: 13.5 us -> 0.78 us
    all_gather x1 -> x0, waiting for transfers between devices: 344 us -> none  [shards(): lax.all_gather(weighted, 'stn', axis=2, tiled=True)]
    ppermute x0 -> x57, waiting for transfers between devices: none -> 317 us  [swapped(): lax.ppermute(block, axis, [(i, i ^ mask) for i in range(lax.axis_size(axi...]
    ppermute x0 -> x57, starting transfers between devices: none -> 195 us  [swapped(): lax.ppermute(block, axis, [(i, i ^ mask) for i in range(lax.axis_size(axi...]
    all_to_all x1 -> x0, waiting for transfers between devices: 166 us -> none  [shards(): lax.all_to_all(spectra, 'chan', split_axis=0, concat_axis=2, tiled=True)]
    dot_general x2 -> x0, matrix products: 146 us -> none  [the longest x1 84.3 us: shards(): jnp.einsum('qn,stn->qst', dft_table(length), filtered, preferred_element_...]
    pallas_call x0 -> x16, Pallas kernels: none -> 128 us  [the longest x2 52.4 us: spectra(): pl.pallas_call(functools.partial(spectra_kernel, start, count, halo is no...]
    all_to_all x1 -> x0, starting transfers between devices: 82.2 us -> none  [shards(): lax.all_to_all(spectra, 'chan', split_axis=0, concat_axis=2, tiled=True)]
    div x1 -> x0, local copies, waits for them, and re-layouts: 62.6 us -> none  [cross_tile(): return jnp.stack([real_part, imag_part], axis=1) / count]
  transfers between devices with their start and end apart: 3 -> 58, of which waited for: 3 -> 26; matrix products, arithmetic and copies ran while one was open for 6% -> 5% of each run, Pallas kernels for 0% -> 15%
where the time goes in v1:
time: 704 us; the launch traced here: 693 us
  waiting for transfers between devices  317 us (45%)
  starting transfers between devices  201 us (29%)
  Pallas kernels  128 us (18%)
  local copies, waits for them, and re-layouts  43.6 us (6%)
    ppermute x57, waiting for transfers between devices, swapped(): lax.ppermute(block, axis, [(i, i ^ mask) for i in range(lax.axis_size(axi...  317 us
    ppermute x57, starting transfers between devices, swapped(): lax.ppermute(block, axis, [(i, i ^ mask) for i in range(lax.axis_size(axi...  195 us
    pallas_call x2, Pallas kernels, spectra(): pl.pallas_call(functools.partial(spectra_kernel, start, count, halo is no...  52.4 us
    pallas_call x2, Pallas kernels, correlated(): pl.pallas_call(functools.partial(correlate_kernel, parts, widths, scale),...  43.9 us
    pallas_call x12, Pallas kernels, joined(): pl.pallas_call(functools.partial(join_kernel, count), grid=(chans // grou...  31.7 us
  transfers between devices with their start and end apart: 58, of which 26 were waited for; matrix products, arithmetic and copies ran while one was open for 5% of the time, Pallas kernels for 15%

profile of v1, /device:TPU:0, one launch (start us, length us, event | category | flops | bytes accessed | tf_op | source)
XLA Modules:
  0.0 693.0 jit_solution(13269601391585392647)
XLA Ops:
  14.3 18.3 %shard_map.46 = (bf16[256,512]{1,0:T(8,128)(2,1)}, bf16[256,512]{1,0:T(8,128)(2,1)}, bf16[256,512]{1,0:T(8,128)(2,1)}, bf16[256,512]{1,0:T(8,128)(2,1)}, bf16[25...) custom-call(bf16[512,12288]{1,0:T(8,128)(2,1)} %refs_1_.3, ...), custom_call_target="tpu_custom_call" | custom-call | flops 10737418240 | bytes 16777216 | tf_op jit(solution)/shard_map/pallas_call | solution.py:94
  46.2 9.0 %broadcast_in_dim.36 = f32[16,48,256,2]{0,3,2,1:T(2,128)} broadcast(f32[16,48,256]{0,2,1:T(8,128)} %copy.14), dimensions={0,1,2} | broadcast | bytes 2359296 | tf_op jit(solution)/shard_map/broadcast_in_dim | solution.py:242
  55.2 7.4 %copy.15 = f32[16,16,3,512]{3,0,2,1:T(8,128)S(1)} copy(f32[16,16,3,512]{0,3,2,1:T(8,128)} %bitcast.21) | data formatting | bytes 3145728 | tf_op jit(solution)/shard_map/reshape;reshape | solution.py:243
  64.2 76.7 %collective-permute-start.9 = (bf16[256,512]{1,0:T(8,128)(2,1)}, bf16[256,512]{1,0:T(8,128)(2,1)S(1)}, u32[]{:S(2)}, u32[]{:S(2)}) collective-permute-start(bf16[256,512]{1,0:T(8,128)(2,1)} %get-tuple-element.65), channel_id=1, source_target_pairs={{0,20},{2,22},{4,16},{6,18},{8,28},{10,30},{12,24},{14,26},{16,4},... | collective-permute-start | bytes 786440 | tf_op jit(solution)/shard_map/ppermute | solution.py:28
  144.0 36.8 %collective-permute-done.9.refs_2_ = bf16[256,512]{1,0:T(8,128)(2,1)S(1)} collective-permute-done((bf16[256,512]{1,0:T(8,128)(2,1)}, bf16[256,512]{1,0:T(8,128)(2,1)S(1)}, u32[]{:S(2)}, u32[]{:S(2)}) %collective-permute-start.9) | collective-permute-done | bytes 262176 | tf_op jit(solution)/shard_map/ppermute | solution.py:28
  183.1 7.6 %collective-permute-start.14 = (bf16[256,512]{1,0:T(8,128)(2,1)S(1)}, bf16[256,512]{1,0:T(8,128)(2,1)S(1)}, u32[]{:S(2)}, u32[]{:S(2)}) collective-permute-start(bf16[256,512]{1,0:T(8,128)(2,1)S(1)} %copy-done.55), channel_id=1, source_target_pairs={{0,30},{2,28},{4,26},{6,24},{8,22},{10,20},{12,18},{14,16},{16,14}... | collective-permute-start | bytes 786440 | tf_op jit(solution)/shard_map/ppermute | solution.py:28
  207.7 34.1 %shard_map.51 = (bf16[256,512]{1,0:T(8,128)(2,1)}, bf16[256,512]{1,0:T(8,128)(2,1)}, bf16[256,512]{1,0:T(8,128)(2,1)}, bf16[256,512]{1,0:T(8,128)(2,1)}, bf16[25...) custom-call(bf16[512,7680]{1,0:T(8,128)(2,1)} %collective-permute-do, ...), custom_call_target="tpu_custom_call" | custom-call | flops 21474836480 | bytes 16777216 | tf_op jit(solution)/shard_map/pallas_call | solution.py:94
  249.4 16.2 %collective-permute-start.19 = (bf16[256,512]{1,0:T(8,128)(2,1)}, bf16[256,512]{1,0:T(8,128)(2,1)S(1)}, u32[]{:S(2)}, u32[]{:S(2)}) collective-permute-start(bf16[256,512]{1,0:T(8,128)(2,1)} %get-tuple-element.75), channel_id=1, source_target_pairs={{0,8},{2,10},{4,12},{6,14},{8,0},{10,2},{12,4},{14,6},{16,24},{18,... | collective-permute-start | bytes 786440 | tf_op jit(solution)/shard_map/ppermute | solution.py:28
  271.8 16.2 %collective-permute-start.20 = (bf16[256,512]{1,0:T(8,128)(2,1)}, bf16[256,512]{1,0:T(8,128)(2,1)S(1)}, u32[]{:S(2)}, u32[]{:S(2)}) collective-permute-start(bf16[256,512]{1,0:T(8,128)(2,1)} %get-tuple-element.76), channel_id=1, source_target_pairs={{0,10},{2,8},{4,14},{6,12},{8,2},{10,0},{12,6},{14,4},{16,26},{18,... | collective-permute-start | bytes 786440 | tf_op jit(solution)/shard_map/ppermute | solution.py:28
  296.4 15.9 %collective-permute-done.21.refs_2_ = bf16[256,512]{1,0:T(8,128)(2,1)S(1)} collective-permute-done((bf16[256,512]{1,0:T(8,128)(2,1)}, bf16[256,512]{1,0:T(8,128)(2,1)S(1)}, u32[]{:S(2)}, u32[]{:S(2)}) %collective-permute-start.21) | collective-permute-done | bytes 262176 | tf_op jit(solution)/shard_map/ppermute | solution.py:28
  341.0 14.3 %collective-permute-done.44.refs_2_ = bf16[256,512]{1,0:T(8,128)(2,1)S(1)} collective-permute-done((bf16[256,512]{1,0:T(8,128)(2,1)}, bf16[256,512]{1,0:T(8,128)(2,1)S(1)}, u32[]{:S(2)}, u32[]{:S(2)}) %collective-permute-start.44) | collective-permute-done | bytes 262176 | tf_op jit(solution)/shard_map/ppermute | solution.py:28
  364.1 21.5 %collective-permute-done.47.refs_1_ = bf16[256,512]{1,0:T(8,128)(2,1)S(1)} collective-permute-done((bf16[256,512]{1,0:T(8,128)(2,1)}, bf16[256,512]{1,0:T(8,128)(2,1)S(1)}, u32[]{:S(2)}, u32[]{:S(2)}) %collective-permute-start.47) | collective-permute-done | bytes 262176 | tf_op jit(solution)/shard_map/ppermute | solution.py:28
  385.6 12.9 %collective-permute-done.48.refs_2_ = bf16[256,512]{1,0:T(8,128)(2,1)S(1)} collective-permute-done((bf16[256,512]{1,0:T(8,128)(2,1)}, bf16[256,512]{1,0:T(8,128)(2,1)S(1)}, u32[]{:S(2)}, u32[]{:S(2)}) %collective-permute-start.48) | collective-permute-done | bytes 262176 | tf_op jit(solution)/shard_map/ppermute | solution.py:28
  404.9 13.4 %collective-permute-start.28 = (bf16[256,512]{1,0:T(8,128)(2,1)}, bf16[256,512]{1,0:T(8,128)(2,1)}, u32[]{:S(2)}, u32[]{:S(2)}) collective-permute-start(bf16[256,512]{1,0:T(8,128)(2,1)} %get-tuple-element.84), channel_id=1, source_target_pairs={{0,26},{2,24},{4,30},{6,28},{8,18},{10,16},{12,22},{14,20},{16,10}... | collective-permute-start | bytes 786440 | tf_op jit(solution)/shard_map/ppermute | solution.py:28
  441.3 24.2 %collective-permute-done.26.refs_3_ = bf16[256,512]{1,0:T(8,128)(2,1)} collective-permute-done((bf16[256,512]{1,0:T(8,128)(2,1)}, bf16[256,512]{1,0:T(8,128)(2,1)}, u32[]{:S(2)}, u32[]{:S(2)}) %collective-permute-start.26) | collective-permute-done | bytes 262176 | tf_op jit(solution)/shard_map/ppermute | solution.py:28
  493.0 21.1 %collective-permute-done.57.refs_15_ = bf16[8,2,64,512]{3,2,1,0:T(8,128)(2,1)} collective-permute-done((bf16[8,2,64,512]{3,2,1,0:T(8,128)(2,1)}, bf16[8,2,64,512]{3,2,1,0:T(8,128)(2,1)}, u32[]{:S(2)}, u32[]{:S(2)}) %collective-permute-start.57) | collective-permute-done | bytes 1048608 | tf_op jit(solution)/shard_map/ppermute | solution.py:28
  515.5 21.0 %collective-permute-done.56.refs_14_ = bf16[8,2,64,512]{3,2,1,0:T(8,128)(2,1)} collective-permute-done((bf16[8,2,64,512]{3,2,1,0:T(8,128)(2,1)}, bf16[8,2,64,512]{3,2,1,0:T(8,128)(2,1)}, u32[]{:S(2)}, u32[]{:S(2)}) %collective-permute-start.56) | collective-permute-done | bytes 1048608 | tf_op jit(solution)/shard_map/ppermute | solution.py:28
  538.0 21.0 %collective-permute-done.55.refs_13_ = bf16[8,2,64,512]{3,2,1,0:T(8,128)(2,1)} collective-permute-done((bf16[8,2,64,512]{3,2,1,0:T(8,128)(2,1)}, bf16[8,2,64,512]{3,2,1,0:T(8,128)(2,1)}, u32[]{:S(2)}, u32[]{:S(2)}) %collective-permute-start.55) | collective-permute-done | bytes 1048608 | tf_op jit(solution)/shard_map/ppermute | solution.py:28
  560.5 21.0 %collective-permute-done.54.refs_12_ = bf16[8,2,64,512]{3,2,1,0:T(8,128)(2,1)} collective-permute-done((bf16[8,2,64,512]{3,2,1,0:T(8,128)(2,1)S(1)}, bf16[8,2,64,512]{3,2,1,0:T(8,128)(2,1)}, u32[]{:S(2)}, u32[]{:S(2)}) %collective-permute-start.54) | collective-permute-done | bytes 1048608 | tf_op jit(solution)/shard_map/ppermute | solution.py:28
  581.5 21.9 %shard_map.60.refs_16_ = f32[16,2,512,1024]{3,2,1,0:T(8,128)} custom-call(s32[2]{0:T(128)} %xor_multiply_fusion.place_ref, bf16[16,2,32,512]{3,2,1,0:T(8,128)(2,1)} %shard_map.47.refs_0_, bf16[16,2,32,512]{3,2,1,0:T(8,128)(2,1)} %shard_map.48.refs_1_, bf16[16,2,32,512]{3,2,1,0:T(8,128)(2,1)} %shard_map.49.refs_2_, ...), custom_call_target="tpu_custom_call" | custom-call | flops 12884901888 | bytes 33554432 | tf_op jit(solution)/shard_map/pallas_call | solution.py:191
  603.8 22.5 %collective-permute-done.37.refs_14_ = bf16[8,2,64,512]{3,2,1,0:T(8,128)(2,1)S(1)} collective-permute-done((bf16[8,2,64,512]{3,2,1,0:T(8,128)(2,1)}, bf16[8,2,64,512]{3,2,1,0:T(8,128)(2,1)S(1)}, u32[]{:S(2)}, u32[]{:S(2)}) %collective-permute-start.37) | collective-permute-done | bytes 1048608 | tf_op jit(solution)/shard_map/ppermute | solution.py:28
  626.3 22.5 %collective-permute-done.36.refs_13_ = bf16[8,2,64,512]{3,2,1,0:T(8,128)(2,1)S(1)} collective-permute-done((bf16[8,2,64,512]{3,2,1,0:T(8,128)(2,1)S(1)}, bf16[8,2,64,512]{3,2,1,0:T(8,128)(2,1)S(1)}, u32[]{:S(2)}, u32[]{:S(2)}) %collective-permute-start.36) | collective-permute-done | bytes 1048608 | tf_op jit(solution)/shard_map/ppermute | solution.py:28
  648.8 22.1 %collective-permute-done.35.refs_12_ = bf16[8,2,64,512]{3,2,1,0:T(8,128)(2,1)} collective-permute-done((bf16[8,2,64,512]{3,2,1,0:T(8,128)(2,1)S(1)}, bf16[8,2,64,512]{3,2,1,0:T(8,128)(2,1)}, u32[]{:S(2)}, u32[]{:S(2)}) %collective-permute-start.35) | collective-permute-done | bytes 1048608 | tf_op jit(solution)/shard_map/ppermute | solution.py:28
  670.9 22.0 %shard_map.61 = f32[16,2,512,1024]{3,2,1,0:T(8,128)} custom-call(s32[2]{0:T(128)} %xor_multiply_fusion.place_ref, bf16[16,2,32,512]{3,2,1,0:T(8,128)(2,1)} %shard_map.47.refs_0_, bf16[16,2,32,512]{3,2,1,0:T(8,128)(2,1)} %shard_map.48.refs_1_, bf16[16,2,32,512]{3,2,1,0:T(8,128)(2,1)} %shard_map.49.refs_2_, ...), custom_call_target="tpu_custom_call", output_to_operand_aliasing={{}: (17, {})} | custom-call | flops 12884901888 | bytes 33554432 | tf_op jit(solution)/shard_map/pallas_call | solution.py:191
  (261 shorter events, 172.8 us)
Async XLA Ops:
  6.9 199.5 %collective-permute-start.15 = (bf16[512,7680]{1,0:T(8,128)(2,1)}, bf16[512,7680]{1,0:T(8,128)(2,1)}, u32[]{:S(2)}, u32[]{:S(2)}) collective-permute-start(bf16[512,7680]{1,0:T(8,128)(2,1)} %slice.58), channel_id=1, source_target_pairs={{0,2},{2,4},{4,6},{6,8},{8,10},{10,12},{12,14},{14,16},{16,18},{18... | collective-permute-start | bytes 23592968 | tf_op jit(solution)/shard_map/ppermute | solution.py:24
  36.0 104.9 %collective-permute-start.6 = (bf16[256,512]{1,0:T(8,128)(2,1)}, bf16[256,512]{1,0:T(8,128)(2,1)}, u32[]{:S(2)}, u32[]{:S(2)}) collective-permute-start(bf16[256,512]{1,0:T(8,128)(2,1)} %get-tuple-element.62), channel_id=1, source_target_pairs={{0,14},{2,12},{4,10},{6,8},{8,6},{10,4},{12,2},{14,0},{16,30},{18,... | collective-permute-start | bytes 786440 | tf_op jit(solution)/shard_map/ppermute | solution.py:28
  42.1 98.8 %collective-permute-start.7 = (bf16[256,512]{1,0:T(8,128)(2,1)}, bf16[256,512]{1,0:T(8,128)(2,1)}, u32[]{:S(2)}, u32[]{:S(2)}) collective-permute-start(bf16[256,512]{1,0:T(8,128)(2,1)} %get-tuple-element.63), channel_id=1, source_target_pairs={{0,16},{2,18},{4,20},{6,22},{8,24},{10,26},{12,28},{14,30},{16,0},... | collective-permute-start | bytes 786440 | tf_op jit(solution)/shard_map/ppermute | solution.py:28
  63.3 80.5 %collective-permute-start.8 = (bf16[256,512]{1,0:T(8,128)(2,1)}, bf16[256,512]{1,0:T(8,128)(2,1)S(1)}, u32[]{:S(2)}, u32[]{:S(2)}) collective-permute-start(bf16[256,512]{1,0:T(8,128)(2,1)} %get-tuple-element.64), channel_id=1, source_target_pairs={{0,18},{2,16},{4,22},{6,20},{8,26},{10,24},{12,30},{14,28},{16,2},... | collective-permute-start | bytes 786440 | tf_op jit(solution)/shard_map/ppermute | solution.py:28
  64.2 116.6 %collective-permute-start.9 = (bf16[256,512]{1,0:T(8,128)(2,1)}, bf16[256,512]{1,0:T(8,128)(2,1)S(1)}, u32[]{:S(2)}, u32[]{:S(2)}) collective-permute-start(bf16[256,512]{1,0:T(8,128)(2,1)} %get-tuple-element.65), channel_id=1, source_target_pairs={{0,20},{2,22},{4,16},{6,18},{8,28},{10,30},{12,24},{14,26},{16,4},... | collective-permute-start | bytes 786440 | tf_op jit(solution)/shard_map/ppermute | solution.py:28
  143.9 61.7 %collective-permute-start = (bf16[256,512]{1,0:T(8,128)(2,1)S(1)}, bf16[256,512]{1,0:T(8,128)(2,1)S(1)}, u32[]{:S(2)}, u32[]{:S(2)}) collective-permute-start(bf16[256,512]{1,0:T(8,128)(2,1)S(1)} %copy-done.54), channel_id=1, source_target_pairs={{0,2},{2,0},{4,6},{6,4},{8,10},{10,8},{12,14},{14,12},{16,18},{18,... | collective-permute-start | bytes 786440 | tf_op jit(solution)/shard_map/ppermute | solution.py:28
  206.4 65.4 %collective-permute-start.32 = (bf16[16,2,32,512]{3,2,1,0:T(8,128)(2,1)S(1)}, bf16[16,2,32,512]{3,2,1,0:T(8,128)(2,1)S(1)}, u32[]{:S(2)}, u32[]{:S(2)}) collective-permute-start(bf16[16,2,32,512]{3,2,1,0:T(8,128)(2,1)S(1)} %copy-done), channel_id=1, source_target_pairs={{0,1},{1,0},{2,3},{3,2},{4,5},{5,4},{6,7},{7,6},{8,9},{9,8},{10,11... | collective-permute-start | bytes 3145736 | tf_op jit(solution)/shard_map/ppermute | solution.py:28
  241.8 46.2 %collective-permute-start.16 = (bf16[256,512]{1,0:T(8,128)(2,1)}, bf16[256,512]{1,0:T(8,128)(2,1)S(1)}, u32[]{:S(2)}, u32[]{:S(2)}) collective-permute-start(bf16[256,512]{1,0:T(8,128)(2,1)} %get-tuple-element.72), channel_id=1, source_target_pairs={{0,2},{2,0},{4,6},{6,4},{8,10},{10,8},{12,14},{14,12},{16,18},{18,... | collective-permute-start | bytes 786440 | tf_op jit(solution)/shard_map/ppermute | solution.py:28
  242.7 46.8 %collective-permute-start.17 = (bf16[256,512]{1,0:T(8,128)(2,1)}, bf16[256,512]{1,0:T(8,128)(2,1)S(1)}, u32[]{:S(2)}, u32[]{:S(2)}) collective-permute-start(bf16[256,512]{1,0:T(8,128)(2,1)} %get-tuple-element.73), channel_id=1, source_target_pairs={{0,4},{2,6},{4,0},{6,2},{8,12},{10,14},{12,8},{14,10},{16,20},{18,... | collective-permute-start | bytes 786440 | tf_op jit(solution)/shard_map/ppermute | solution.py:28
  337.7 47.9 %collective-permute-start.47 = (bf16[256,512]{1,0:T(8,128)(2,1)}, bf16[256,512]{1,0:T(8,128)(2,1)S(1)}, u32[]{:S(2)}, u32[]{:S(2)}) collective-permute-start(bf16[256,512]{1,0:T(8,128)(2,1)} %get-tuple-element.96), channel_id=1, source_target_pairs={{0,18},{2,16},{4,22},{6,20},{8,26},{10,24},{12,30},{14,28},{16,2},... | collective-permute-start | bytes 786440 | tf_op jit(solution)/shard_map/ppermute | solution.py:28
  339.8 58.8 %collective-permute-start.48 = (bf16[256,512]{1,0:T(8,128)(2,1)}, bf16[256,512]{1,0:T(8,128)(2,1)S(1)}, u32[]{:S(2)}, u32[]{:S(2)}) collective-permute-start(bf16[256,512]{1,0:T(8,128)(2,1)} %get-tuple-element.97), channel_id=1, source_target_pairs={{0,20},{2,22},{4,16},{6,18},{8,28},{10,30},{12,24},{14,26},{16,4},... | collective-permute-start | bytes 786440 | tf_op jit(solution)/shard_map/ppermute | solution.py:28
  355.3 48.3 %collective-permute-start.49 = (bf16[256,512]{1,0:T(8,128)(2,1)}, bf16[256,512]{1,0:T(8,128)(2,1)S(1)}, u32[]{:S(2)}, u32[]{:S(2)}) collective-permute-start(bf16[256,512]{1,0:T(8,128)(2,1)} %get-tuple-element.98), channel_id=1, source_target_pairs={{0,22},{2,20},{4,18},{6,16},{8,30},{10,28},{12,26},{14,24},{16,6},... | collective-permute-start | bytes 786440 | tf_op jit(solution)/shard_map/ppermute | solution.py:28
  403.6 61.9 %collective-permute-start.26 = (bf16[256,512]{1,0:T(8,128)(2,1)}, bf16[256,512]{1,0:T(8,128)(2,1)}, u32[]{:S(2)}, u32[]{:S(2)}) collective-permute-start(bf16[256,512]{1,0:T(8,128)(2,1)} %get-tuple-element.82), channel_id=1, source_target_pairs={{0,22},{2,20},{4,18},{6,16},{8,30},{10,28},{12,26},{14,24},{16,6},... | collective-permute-start | bytes 786440 | tf_op jit(solution)/shard_map/ppermute | solution.py:28
  403.6 63.4 %collective-permute-start.27 = (bf16[256,512]{1,0:T(8,128)(2,1)}, bf16[256,512]{1,0:T(8,128)(2,1)}, u32[]{:S(2)}, u32[]{:S(2)}) collective-permute-start(bf16[256,512]{1,0:T(8,128)(2,1)} %get-tuple-element.83), channel_id=1, source_target_pairs={{0,24},{2,26},{4,28},{6,30},{8,16},{10,18},{12,20},{14,22},{16,8},... | collective-permute-start | bytes 786440 | tf_op jit(solution)/shard_map/ppermute | solution.py:28
  404.9 62.6 %collective-permute-start.28 = (bf16[256,512]{1,0:T(8,128)(2,1)}, bf16[256,512]{1,0:T(8,128)(2,1)}, u32[]{:S(2)}, u32[]{:S(2)}) collective-permute-start(bf16[256,512]{1,0:T(8,128)(2,1)} %get-tuple-element.84), channel_id=1, source_target_pairs={{0,26},{2,24},{4,30},{6,28},{8,18},{10,16},{12,22},{14,20},{16,10}... | collective-permute-start | bytes 786440 | tf_op jit(solution)/shard_map/ppermute | solution.py:28
  418.3 50.7 %collective-permute-start.29 = (bf16[256,512]{1,0:T(8,128)(2,1)}, bf16[256,512]{1,0:T(8,128)(2,1)}, u32[]{:S(2)}, u32[]{:S(2)}) collective-permute-start(bf16[256,512]{1,0:T(8,128)(2,1)} %get-tuple-element.85), channel_id=1, source_target_pairs={{0,28},{2,30},{4,24},{6,26},{8,20},{10,22},{12,16},{14,18},{16,12}... | collective-permute-start | bytes 786440 | tf_op jit(solution)/shard_map/ppermute | solution.py:28
  467.0 47.0 %collective-permute-start.57 = (bf16[8,2,64,512]{3,2,1,0:T(8,128)(2,1)}, bf16[8,2,64,512]{3,2,1,0:T(8,128)(2,1)}, u32[]{:S(2)}, u32[]{:S(2)}) collective-permute-start(bf16[8,2,64,512]{3,2,1,0:T(8,128)(2,1)} %shard_map.59.refs_7_), channel_id=1, source_target_pairs={{0,1},{1,0},{2,3},{3,2},{4,5},{5,4},{6,7},{7,6},{8,9},{9,8},{10,11... | collective-permute-start | bytes 3145736 | tf_op jit(solution)/shard_map/ppermute | solution.py:28
  467.5 69.0 %collective-permute-start.56 = (bf16[8,2,64,512]{3,2,1,0:T(8,128)(2,1)}, bf16[8,2,64,512]{3,2,1,0:T(8,128)(2,1)}, u32[]{:S(2)}, u32[]{:S(2)}) collective-permute-start(bf16[8,2,64,512]{3,2,1,0:T(8,128)(2,1)} %shard_map.58.refs_6_), channel_id=1, source_target_pairs={{0,1},{1,0},{2,3},{3,2},{4,5},{5,4},{6,7},{7,6},{8,9},{9,8},{10,11... | collective-permute-start | bytes 3145736 | tf_op jit(solution)/shard_map/ppermute | solution.py:28
  469.0 90.0 %collective-permute-start.55 = (bf16[8,2,64,512]{3,2,1,0:T(8,128)(2,1)}, bf16[8,2,64,512]{3,2,1,0:T(8,128)(2,1)}, u32[]{:S(2)}, u32[]{:S(2)}) collective-permute-start(bf16[8,2,64,512]{3,2,1,0:T(8,128)(2,1)} %shard_map.57.refs_5_), channel_id=1, source_target_pairs={{0,1},{1,0},{2,3},{3,2},{4,5},{5,4},{6,7},{7,6},{8,9},{9,8},{10,11... | collective-permute-start | bytes 3145736 | tf_op jit(solution)/shard_map/ppermute | solution.py:28
  469.6 111.9 %collective-permute-start.54 = (bf16[8,2,64,512]{3,2,1,0:T(8,128)(2,1)S(1)}, bf16[8,2,64,512]{3,2,1,0:T(8,128)(2,1)}, u32[]{:S(2)}, u32[]{:S(2)}) collective-permute-start(bf16[8,2,64,512]{3,2,1,0:T(8,128)(2,1)S(1)} %copy-done.8), channel_id=1, source_target_pairs={{0,1},{1,0},{2,3},{3,2},{4,5},{5,4},{6,7},{7,6},{8,9},{9,8},{10,11... | collective-permute-start | bytes 3145736 | tf_op jit(solution)/shard_map/ppermute | solution.py:28
  491.5 112.4 %collective-permute-start.38 = (bf16[8,2,64,512]{3,2,1,0:T(8,128)(2,1)}, bf16[8,2,64,512]{3,2,1,0:T(8,128)(2,1)S(1)}, u32[]{:S(2)}, u32[]{:S(2)}) collective-permute-start(bf16[8,2,64,512]{3,2,1,0:T(8,128)(2,1)} %shard_map.55.refs_7_), channel_id=1, source_target_pairs={{0,1},{1,0},{2,3},{3,2},{4,5},{5,4},{6,7},{7,6},{8,9},{9,8},{10,11... | collective-permute-start | bytes 3145736 | tf_op jit(solution)/shard_map/ppermute | solution.py:28
  514.0 112.2 %collective-permute-start.37 = (bf16[8,2,64,512]{3,2,1,0:T(8,128)(2,1)}, bf16[8,2,64,512]{3,2,1,0:T(8,128)(2,1)S(1)}, u32[]{:S(2)}, u32[]{:S(2)}) collective-permute-start(bf16[8,2,64,512]{3,2,1,0:T(8,128)(2,1)} %shard_map.54.refs_6_), channel_id=1, source_target_pairs={{0,1},{1,0},{2,3},{3,2},{4,5},{5,4},{6,7},{7,6},{8,9},{9,8},{10,11... | collective-permute-start | bytes 3145736 | tf_op jit(solution)/shard_map/ppermute | solution.py:28
  536.5 112.2 %collective-permute-start.36 = (bf16[8,2,64,512]{3,2,1,0:T(8,128)(2,1)S(1)}, bf16[8,2,64,512]{3,2,1,0:T(8,128)(2,1)S(1)}, u32[]{:S(2)}, u32[]{:S(2)}) collective-permute-start(bf16[8,2,64,512]{3,2,1,0:T(8,128)(2,1)S(1)} %copy-done.10), channel_id=1, source_target_pairs={{0,1},{1,0},{2,3},{3,2},{4,5},{5,4},{6,7},{7,6},{8,9},{9,8},{10,11... | collective-permute-start | bytes 3145736 | tf_op jit(solution)/shard_map/ppermute | solution.py:28
  559.0 111.9 %collective-permute-start.35 = (bf16[8,2,64,512]{3,2,1,0:T(8,128)(2,1)S(1)}, bf16[8,2,64,512]{3,2,1,0:T(8,128)(2,1)}, u32[]{:S(2)}, u32[]{:S(2)}) collective-permute-start(bf16[8,2,64,512]{3,2,1,0:T(8,128)(2,1)S(1)} %copy-done.9), channel_id=1, source_target_pairs={{0,1},{1,0},{2,3},{3,2},{4,5},{5,4},{6,7},{7,6},{8,9},{9,8},{10,11... | collective-permute-start | bytes 3145736 | tf_op jit(solution)/shard_map/ppermute | solution.py:28
  (93 other events, 4533.6 us)

commit v2 on v0

v2 whole, which is shorter than its diff:
```python
import functools
import math

import jax
import jax.numpy as jnp
import numpy as np
from jax import lax
from jax.experimental import pallas as pl
from jax.experimental.pallas import tpu as pltpu
from jax.sharding import PartitionSpec as P

POLS = 2
LANES = 128
ROWS = 16
STEP = 8
VMEM = 56 * 1024 * 1024
BF16 = jnp.bfloat16
F32 = jnp.float32


def shifted(block, axis, distance):
    devices = range(lax.axis_size(axis))
    route = [(i - distance, i) for i in devices if i - distance in devices]
    return lax.ppermute(block, axis, route)


def swapped(block, axis, mask):
    return lax.ppermute(block, axis, [(i, i ^ mask) for i in range(lax.axis_size(axis))])


def dft_table(length):
    rows_index = np.arange(length)
    phase = (rows_index // 2)[:, None] * np.arange(length)[None, :] % length
    angles = phase.astype(np.float32) * np.float32(2.0 * math.pi / length)
    values = np.where((rows_index % 2 == 0)[:, None], np.cos(angles), -np.sin(angles))
    return (values / np.float32(math.sqrt(length))).astype(np.float32)


def spectra_kernel(start, count, halos, *refs):
    halo_refs, refs = refs[:halos], refs[halos:]
    volts_ref, taps_ref, table_ref = refs[:3]
    outs, (filt_ref, res_ref) = refs[3:-2], refs[-2:]
    taps, length = taps_ref.shape
    signals = volts_ref.shape[0]

    def frame(rows, j, n0):
        if j < 0:
            piece, at = divmod(j + taps - 1, (taps - 1) // halos)
            return halo_refs[piece][rows, pl.ds(at * length + n0, LANES)].astype(F32)
        return volts_ref[rows, pl.ds(j * length + n0, LANES)].astype(F32)

    def body(g, carry):
        rows = pl.ds(pl.multiple_of(g * ROWS, ROWS), ROWS)
        for n0 in range(0, length, LANES):
            coef = [taps_ref[k : k + 1, n0 : n0 + LANES] for k in range(taps)]
            for t0 in range(0, count, STEP):
                sums = [None] * STEP
                for j in range(start + t0 - (taps - 1), start + t0 + STEP):
                    value = frame(rows, j, n0)
                    for t in range(STEP):
                        k = start + t0 + t - j
                        if 0 <= k < taps:
                            term = coef[k] * value
                            sums[t] = term if sums[t] is None else sums[t] + term
                for t in range(STEP):
                    filt_ref[t0 + t, rows, n0 : n0 + LANES] = sums[t].astype(BF16)
        return carry

    lax.fori_loop(0, signals // ROWS, body, 0)
    for t in range(count):
        res_ref[pl.ds(t, length, stride=count), :] = lax.dot_general(
            table_ref[...], filt_ref[t], (((1,), (1,)), ((), ())), preferred_element_type=F32
        )
    at = 0
    for out in outs:
        out[...] = res_ref[at : at + out.shape[0], :].astype(BF16)
        at += out.shape[0]


def spectra(volts, halos, taps, table, start, count, rows, begin, signals):
    length = taps.shape[1]
    block = min(LANES, signals)
    width = (start + count) * length
    in_specs = [
        pl.BlockSpec((block, width), lambda s: (s + begin // block, 0)),
        pl.BlockSpec(taps.shape, lambda s: (0, 0)),
        pl.BlockSpec(table.shape, lambda s: (0, 0)),
    ]
    args = [*halos, volts, taps, table]
    in_specs = [pl.BlockSpec((block, halo.shape[1]), lambda s: (s, 0)) for halo in halos] + in_specs
    return pl.pallas_call(
        functools.partial(spectra_kernel, start, count, len(halos)),
        grid=(signals // block,),
        in_specs=in_specs,
        out_specs=[pl.BlockSpec((n * count, block), lambda s: (0, s)) for n in rows],
        out_shape=[jax.ShapeDtypeStruct((n * count, signals), BF16) for n in rows],
        scratch_shapes=[
            pltpu.VMEM((count, block, length), BF16),
            pltpu.VMEM((length * count, block), F32),
        ],
        compiler_params=pltpu.CompilerParams(vmem_limit_bytes=VMEM),
        cost_estimate=pl.CostEstimate(
            flops=2 * length * length * count * signals * 5,
            bytes_accessed=2 * signals * (width + length * count),
            transcendentals=0,
        ),
    )(*args)


def join_kernel(count, pieces, *refs):
    held, outs = refs[:pieces], refs[pieces:]
    chans = outs[0].shape[0]
    for m, out in enumerate(outs):
        for c in range(chans):
            values = [
                piece[((m * chans + c) * 2) * count : ((m * chans + c) * 2 + 2) * count, :].astype(F32)
                for piece in held
            ]
            for r in range(2):
                part = [value[r * count : (r + 1) * count] for value in values]
                out[c, r] = jnp.concatenate(part, axis=0).astype(BF16)


def joined(held, outputs, count):
    pieces = len(held)
    rows, signals = held[0].shape
    chans = rows // (outputs * 2 * count)
    block = min(LANES, signals)
    shape = (chans, 2, pieces * count)
    return pl.pallas_call(
        functools.partial(join_kernel, count, pieces),
        grid=(signals // block,),
        in_specs=[pl.BlockSpec((rows, block), lambda s: (0, s))] * pieces,
        out_specs=[pl.BlockSpec(shape + (block,), lambda s: (0, 0, 0, s))] * outputs,
        out_shape=[jax.ShapeDtypeStruct(shape + (signals,), BF16)] * outputs,
        compiler_params=pltpu.CompilerParams(vmem_limit_bytes=VMEM),
        cost_estimate=pl.CostEstimate(
            flops=pieces * rows * signals, bytes_accessed=4 * pieces * rows * signals, transcendentals=0
        ),
    )(*held)


class Block:
    def __init__(self, array, start, count, sources, column, channel):
        self.array, self.start, self.count, self.sources = array, start, count, sources
        self.column, self.channel = column, channel


def correlate_kernel(layout, scale, place_ref, *refs):
    (out_ref, token_ref), (lhs_re, lhs_im, rhs) = refs[-5:-3], refs[-3:]
    token_ref[...] = jnp.zeros_like(token_ref)
    total = rhs.shape[0] // 2
    sides, width, frames = layout["sides"], layout["width"], layout["frames"]
    blocks = layout["blocks"]
    keeps = refs[: sides]
    refs = refs[sides:]
    per = STEP
    for c in range(out_ref.shape[0]):
        for side in range(sides):
            for i, (at, start, count, sources, column, columns) in enumerate(blocks):
                ref = refs[side * len(blocks) + i]
                for r in range(2):
                    values = ref[c, r].astype(F32)
                    rows = []
                    for s, source in enumerate(sources):
                        first = (place_ref[2] ^ source) * (frames // per) + start // per
                        for b in range(count // per):
                            keep = keeps[side][c, pl.ds(first + b, 1), column : column + columns]
                            top = s * count + b * per
                            rows.append(values[top : top + per] * keep)
                    height = count * len(sources)
                    rhs[r * total + at : r * total + at + height, column : column + columns] = jnp.concatenate(
                        rows, axis=0
                    ).astype(BF16)
            if side == 0:
                turned = rhs[...].T
                lhs_re[...] = turned
                lhs_im[:, :total] = turned[:, total:]
                lhs_im[:, total:] = -turned[:, :total]
            columns = pl.ds(pl.multiple_of(place_ref[side] * LANES, LANES), width)
            for r, lhs in enumerate((lhs_re, lhs_im)):
                out_ref[c, r, :, columns] = scale * jnp.dot(lhs[...], rhs[...], preferred_element_type=F32)


def correlated(result, first, chans, local, others, keeps, place, shape, scale, frames, devices):
    step = math.gcd(chans, math.gcd(first, 2))
    signals = shape[2]
    layout = {"sides": len(keeps), "width": signals, "frames": frames, "blocks": []}
    tops, total = {}, 0
    for block in local:
        if block.start not in tops:
            tops[block.start], total = total, total + block.count * devices
        layout["blocks"].append(
            (tops[block.start] + block.sources[0] * block.count, block.start, block.count, block.sources,
             block.column, block.array.shape[3])
        )

    def spec(array, begin):
        return pl.BlockSpec(
            (step,) + array.shape[1:],
            lambda c, place: (c + (first - begin) // step,) + (0,) * (array.ndim - 1),
        )

    in_specs = [spec(keep, 0) for keep in keeps]
    in_specs += [spec(block.array, block.channel) for block in local + others]
    args = list(keeps) + [block.array for block in local + others]
    aliases = {}
    if result is not None:
        in_specs.append(pl.BlockSpec(memory_space=pl.ANY))
        aliases = {1 + len(args): 0}
        args.append(result)
    return pl.pallas_call(
        functools.partial(correlate_kernel, layout, scale),
        grid_spec=pltpu.PrefetchScalarGridSpec(
            num_scalar_prefetch=1,
            grid=(chans // step,),
            in_specs=in_specs,
            out_specs=[
                pl.BlockSpec((step,) + shape[1:], lambda c, place: (c + first // step, 0, 0, 0)),
                pl.BlockSpec((STEP, LANES), lambda c, place: (0, 0)),
            ],
            scratch_shapes=[
                pltpu.VMEM((signals, 2 * total), BF16),
                pltpu.VMEM((signals, 2 * total), BF16),
                pltpu.VMEM((2 * total, signals), BF16),
            ],
        ),
        out_shape=[jax.ShapeDtypeStruct(shape, F32), jax.ShapeDtypeStruct((STEP, LANES), F32)],
        input_output_aliases=aliases,
        compiler_params=pltpu.CompilerParams(vmem_limit_bytes=VMEM),
        cost_estimate=pl.CostEstimate(
            flops=8 * chans * total * signals * shape[3],
            bytes_accessed=4 * chans * 2 * signals * shape[3],
            transcendentals=0,
        ),
    )(place, *args)


def gated(arrays, *tokens):
    n = len(arrays)
    anywhere = pl.BlockSpec(memory_space=pl.ANY)
    return pl.pallas_call(
        lambda *refs: None,
        in_specs=[anywhere] * (n + len(tokens)),
        out_specs=[anywhere] * n,
        out_shape=[jax.ShapeDtypeStruct(array.shape, array.dtype) for array in arrays],
        input_output_aliases={i: i for i in range(n)},
    )(*arrays, *tokens)


class Chunk:
    def __init__(self, near, start, count, column, channel, chans):
        self.near, self.start, self.count, self.column = near, start, count, column
        self.channel, self.chans = channel, chans


def wide_shards(voltages, pfb_taps, flags):
    taps, length = pfb_taps.shape
    signals = voltages.shape[0]
    frames = voltages.shape[1] // length
    devices = lax.axis_size("chan")
    me = lax.axis_index("chan")
    stns = lax.axis_size("stn")
    chans = length // 2 // devices
    total = frames * devices
    early, late = taps, frames - taps
    width = signals // 2

    def halo(half, piece, pieces):
        size = (taps - 1) // pieces * length
        at = (frames - taps + 1) * length + piece * size
        return voltages[half * width : (half + 1) * width, at : at + size]

    halos = [[shifted(halo(0, 0, 1), "chan", 1)], []]

    spread = jnp.repeat(jnp.eye(signals // POLS, dtype=BF16), POLS, axis=1)

    def kept(block):
        return lax.dot_general(block.astype(BF16), spread, (((0,), (0,)), ((), ())), preferred_element_type=F32)

    other_flags = swapped(flags, "stn", 1)
    keeps = [kept(block) for block in (flags, other_flags)]

    table = jnp.asarray(dft_table(length)).astype(BF16).reshape(devices, chans, 2, length)

    def tables(chunks):
        rows = []
        for chunk in chunks:
            order = np.arange(devices).reshape(-1, chunk.near).T.reshape(-1)
            part = jnp.take(table[:, chunk.channel : chunk.channel + chunk.chans], me ^ order, axis=0)
            rows.append(part.reshape(-1, length))
        sizes = [part.shape[0] // chunk.near for part, chunk in zip(rows, chunks) for _ in range(chunk.near)]
        return jnp.concatenate(rows, axis=0), sizes

    chunks = [Chunk(NEARS[0], early, late, 0, 0, chans), Chunk(NEARS[1], 0, early, 0, 0, chans)]
    begin = 0
    for part, close in zip(SPLITS, NEARS[2:]):
        size = chans * part // sum(SPLITS)
        chunks.append(Chunk(close, 0, early, width, begin, size))
        begin += size
    kernels = [(chunks[:1], None, 0, signals), (chunks[1:2], 0, 0, width), (chunks[2:], 1, width, width)]

    sent, ready, arrived, crossed = {}, {}, {}, {}
    def ordered(orders):
        counts = [devices // chunk.near for chunk in chunks]
        return [(k, m) for k, n in enumerate(counts) for m in orders.get(n, range(n))]

    units, issued = ordered(SWAPS), ordered(SENDS)
    first = {}
    for i, (k, m) in enumerate(units):
        first.setdefault(k, i)

    def compute(n, token):
        group, half, column, size = kernels[n]
        rows, sizes = tables(group)
        before = [] if half is None else halos[half]
        if before:
            before = gated(before, token)
        outs = spectra(voltages, before, pfb_taps, rows, group[0].start, group[0].count, sizes, column, size)
        outs = list(outs)
        for chunk in group:
            sent[chunks.index(chunk)] = outs[: chunk.near]
            outs = outs[chunk.near :]

    def near(k):
        sent[k] = [swapped(piece, "chan", s) if s else piece for s, piece in enumerate(sent[k])]

    def join(k):
        for m, block in enumerate(joined(sent[k], devices // chunks[k].near, chunks[k].count)):
            ready[k, m] = block

    def far(k, m):
        arrived[k, m] = swapped(ready[k, m], "chan", m * chunks[k].near) if m else ready[k, m]

    place = (lax.axis_index("stn") ^ jnp.arange(stns, dtype=jnp.int32)) * (signals // LANES)
    place = jnp.concatenate([place, me[None].astype(jnp.int32)])

    def correlate(k, result):
        last = chunks[k]
        local, others = [], []
        for n, m in units:
            chunk = chunks[n]
            if n < 2 or n == k:
                for side, have in ((local, arrived), (others, crossed)):
                    sources = range(m * chunk.near, (m + 1) * chunk.near)
                    side.append(Block(have[n, m], chunk.start, chunk.count, sources, chunk.column, chunk.channel))
        return correlated(
            result, last.channel, last.chans, local, others, keeps, place,
            (chans, 2, signals, signals * stns), 1.0 / total, frames, devices,
        )

    result, marks = None, {}
    compute(0, None)
    near(0)
    join(0)
    token = sent[0][0]
    for u in issued[:AHEAD]:
        far(*u)
    pieces = PIECES if (taps - 1) % PIECES == 0 else 1
    for i in range(len(units)):
        for n, (group, half, _, _) in enumerate(kernels):
            if n and max(first[chunks.index(group[0])] - AHEAD - LEAD, 0) == i:
                compute(n, token)
        passed = [(arrived, units[i])]
        nears = [k for k in first if k and first[k] - AHEAD - 2 == i]
        joins = [k for k in first if k and first[k] - AHEAD - 1 == i]
        fars = issued[i + AHEAD : i + AHEAD + 1]
        for k in nears + joins:
            passed += [(sent[k], s) for s in range(len(sent[k]))]
        for u in fars:
            passed.append((ready, u))
        tokens = [token]
        if i >= DEPTH:
            tokens.append(crossed[units[i - DEPTH]])
        if i == 1:
            tokens.append(other_flags)
        for mark in marks.pop(i, []):
            tokens.append(mark)
        outs = list(gated([where[key] for where, key in passed], *tokens))
        for (where, key), out in zip(passed, outs):
            where[key] = out
        token = outs[0]
        for k in nears:
            near(k)
        for k in joins:
            join(k)
        crossed[units[i]] = swapped(arrived[units[i]], "stn", 1)
        for u in fars:
            far(*u)
        if 0 <= FIRST_PIECE <= i < FIRST_PIECE + pieces:
            piece = gated([halo(1, i - FIRST_PIECE, pieces)], token)[0]
            halos[1].append(shifted(piece, "chan", 1))
            marks.setdefault(i + 2, []).append(halos[1][-1])
        for k in first:
            if k >= 2 and k + 1 in first and i == first[k + 1] + LATER:
                result, mark = correlate(k, result)
                marks.setdefault(i + 1, []).append(mark)
    return correlate(len(chunks) - 1, result)[0]


SWAPS = {8: (0, 2, 4, 3, 6, 1, 5, 7), 4: (0, 2, 1, 3)}
SENDS = {8: (0, 2, 4, 3, 6, 1, 5, 7), 4: (0, 2, 1, 3)}
AHEAD = 3
DEPTH = 2
LEAD = 3
NEARS = (2, 4, 4, 4)
SPLITS = (1, 1)
FIRST_PIECE = 4
PIECES = 1
LATER = 3


def cross_tile(local, remote, count):
    prods = jnp.einsum("cpat,cqbt->cpqab", local, remote, preferred_element_type=jnp.float32)
    real_part = prods[:, 0, 0] + prods[:, 1, 1]
    imag_part = prods[:, 1, 0] - prods[:, 0, 1]
    return jnp.stack([real_part, imag_part], axis=1) / count


def narrow_shards(voltages, pfb_taps, flags):
    taps, length = pfb_taps.shape
    signals = voltages.shape[0]
    frames_here = voltages.shape[1] // length
    frames = voltages.reshape(signals, frames_here, length)
    earlier = shifted(frames[:, frames_here - (taps - 1) :, :], "chan", 1)
    padded = jnp.concatenate([earlier, frames], axis=1)
    filtered = jnp.zeros((signals, frames_here, length), F32)
    for k in range(taps):
        offset = taps - 1 - k
        filtered = filtered + pfb_taps[k] * padded[:, offset : offset + frames_here, :]
    filtered = filtered.astype(BF16)
    table = jnp.asarray(dft_table(length)).astype(BF16)
    spectra = jnp.einsum("qn,stn->qst", table, filtered, preferred_element_type=F32).astype(BF16)
    turned = lax.all_to_all(spectra, "chan", split_axis=0, concat_axis=2, tiled=True)
    chans, total = turned.shape[0] // 2, turned.shape[2]
    stations, _, blocks = flags.shape
    keep = jnp.transpose(flags, (1, 0, 2)).astype(BF16)[:, None, :, None, :, None]
    shaped = turned.reshape(chans, 2, stations, POLS, blocks, total // blocks)
    weighted = (shaped * keep).reshape(chans, 2, signals, total)
    return cross_tile(weighted, lax.all_gather(weighted, "stn", axis=2, tiled=True), float(total))


def shards(voltages, pfb_taps, flags):
    if lax.axis_size("stn") != 2 or voltages.shape[0] % (2 * LANES) or lax.axis_size("chan") % NEARS[-1]:
        return narrow_shards(voltages, pfb_taps, flags)
    return wide_shards(voltages, pfb_taps, flags)


def solution(mesh):
    placed = (P("stn", "chan"), P(), P("stn", "chan", None))
    return jax.shard_map(
        shards, mesh=mesh, in_specs=placed, out_specs=P("chan", None, "stn", None), check_vma=False
    )
```

time: 1090 us -> 502 us (0.46)
  waiting for transfers between devices: 514 us -> 197 us
  local copies, waits for them, and re-layouts: 194 us -> 41.9 us
  matrix products: 146 us -> 3.12 us
  other arithmetic: 128 us -> 7.13 us
  Pallas kernels: 0 us -> 115 us
  starting transfers between devices: 87.8 us -> 137 us
  between operations: 13.5 us -> 0.6 us
    all_gather x1 -> x0, waiting for transfers between devices: 344 us -> none  [shards(): lax.all_gather(weighted, 'stn', axis=2, tiled=True)]
    ppermute x0 -> x47, waiting for transfers between devices: none -> 197 us  [swapped(): lax.ppermute(block, axis, [(i, i ^ mask) for i in range(lax.axis_size(axi...]
    all_to_all x1 -> x0, waiting for transfers between devices: 166 us -> none  [shards(): lax.all_to_all(spectra, 'chan', split_axis=0, concat_axis=2, tiled=True)]
    dot_general x2 -> x0, matrix products: 146 us -> none  [the longest x1 84.3 us: shards(): jnp.einsum('qn,stn->qst', dft_table(length), filtered, preferred_element_...]
    ppermute x0 -> x47, starting transfers between devices: none -> 128 us  [swapped(): lax.ppermute(block, axis, [(i, i ^ mask) for i in range(lax.axis_size(axi...]
    pallas_call x0 -> x32, Pallas kernels: none -> 115 us  [the longest x3 55.6 us: spectra(): pl.pallas_call(functools.partial(spectra_kernel, start, count, len(halos)...]
    all_to_all x1 -> x0, starting transfers between devices: 82.2 us -> none  [shards(): lax.all_to_all(spectra, 'chan', split_axis=0, concat_axis=2, tiled=True)]
    div x1 -> x0, local copies, waits for them, and re-layouts: 62.6 us -> none  [cross_tile(): return jnp.stack([real_part, imag_part], axis=1) / count]
  transfers between devices with their start and end apart: 3 -> 49, of which waited for: 3 -> 19; matrix products, arithmetic and copies ran while one was open for 6% -> 5% of each run, Pallas kernels for 0% -> 18%
where the time goes in v2:
time: 502 us; the launch traced here: 501 us
  waiting for transfers between devices  197 us (39%)
  starting transfers between devices  137 us (27%)
  Pallas kernels  115 us (23%)
  local copies, waits for them, and re-layouts  41.9 us (8%)
  other arithmetic  7.13 us (1%)
    ppermute x47, waiting for transfers between devices, swapped(): lax.ppermute(block, axis, [(i, i ^ mask) for i in range(lax.axis_size(axi...  197 us
    ppermute x47, starting transfers between devices, swapped(): lax.ppermute(block, axis, [(i, i ^ mask) for i in range(lax.axis_size(axi...  128 us
    pallas_call x3, Pallas kernels, spectra(): pl.pallas_call(functools.partial(spectra_kernel, start, count, len(halos)...  55.6 us
    pallas_call x2, Pallas kernels, correlated(): pl.pallas_call(functools.partial(correlate_kernel, layout, scale), grid_s...  44.6 us
    unnamed x98, local copies, waits for them, and re-layouts  20.6 us
    pallas_call x4, Pallas kernels, joined(): pl.pallas_call(functools.partial(join_kernel, count, pieces), grid=(signa...  14.4 us
  transfers between devices with their start and end apart: 49, of which 19 were waited for; matrix products, arithmetic and copies ran while one was open for 5% of the time, Pallas kernels for 18%

profile of v2, /device:TPU:0, one launch (start us, length us, event | category | flops | bytes accessed | tf_op | source)
XLA Modules:
  0.0 501.1 jit_solution(14829440923057325925)
XLA Ops:
  0.0 5.8 %fusion.1 = (bf16[256,7680]{1,0:T(8,128)(2,1)}, bf16[256,7680]{1,0:T(8,128)(2,1)}) fusion(bf16[512,12288]{1,0:T(8,128)(2,1)} %refs_1_.5), kind=kLoop, calls=%fused_computation.19 | loop fusion | bytes 15728640 | tf_op jit(solution)/shard_map/slice | solution.py:272
  13.3 18.2 %shard_map.82 = (bf16[2048,512]{1,0:T(8,128)(2,1)}, bf16[2048,512]{1,0:T(8,128)(2,1)}) custom-call(bf16[512,12288]{1,0:T(8,128)(2,1)} %refs_1_.5, f32[16,512]{1,0:T(8,128)} %refs_2_.3, bf16[512,512]{1,0:T(8,128)(2,1)} %reshape.32.refs_2_), custom_call_target="tpu_custom_call" | custom-call | flops 10737418240 | bytes 16777216 | tf_op jit(solution)/shard_map/pallas_call | solution.py:91
  37.6 5.0 %shard_map.83 = (bf16[16,2,16,512]{3,2,1,0:T(8,128)(2,1)}, bf16[16,2,16,512]{3,2,1,0:T(8,128)(2,1)}, bf16[16,2,16,512]{3,2,1,0:T(8,128)(2,1)}, bf16[16,2,16,512]...) custom-call(bf16[2048,512]{1,0:T(8,128)(2,1)} %get-tuple-element.101, ...), custom_call_target="tpu_custom_call" | custom-call | flops 2097152 | bytes 8388608 | tf_op jit(solution)/shard_map/pallas_call | solution.py:130
  57.8 9.7 %collective-permute-done.2.refs_0_ = bf16[16,2,16,512]{3,2,1,0:T(8,128)(2,1)S(1)} collective-permute-done((bf16[16,2,16,512]{3,2,1,0:T(8,128)(2,1)}, bf16[16,2,16,512]{3,2,1,0:T(8,128)(2,1)S(1)}, u32[]{:S(2)}, u32[]{:S(2)}) %collective-permute-start.2) | collective-permute-done | bytes 524320 | tf_op jit(solution)/shard_map/ppermute | solution.py:28
  72.7 18.7 %shard_map.88 = (bf16[2048,256]{1,0:T(8,128)(2,1)}, bf16[2048,256]{1,0:T(8,128)(2,1)}, bf16[2048,256]{1,0:T(8,128)(2,1)}, bf16[2048,256]{1,0:T(8,128)(2,1)}) custom-call(bf16[256,7680]{1,0:T(8,128)(2,1)} %shard_map.87.refs_0_, bf16[512,12288]{1,0:T(8,128)(2,1)} %refs_1_.5, f32[16,512]{1,0:T(8,128)} %refs_2_.3, bf16[512,512]{1,0:T(8,128)(2,1)} %reshape.33.refs_3_), custom_call_target="tpu_custom_call" | custom-call | flops 10737418240 | bytes 8388608 | tf_op jit(solution)/shard_map/pallas_call | solution.py:91
  92.4 11.5 %collective-permute-start.10 = (bf16[2048,256]{1,0:T(8,128)(2,1)}, bf16[2048,256]{1,0:T(8,128)(2,1)S(1)}, u32[]{:S(2)}, u32[]{:S(2)}) collective-permute-start(bf16[2048,256]{1,0:T(8,128)(2,1)} %get-tuple-element.122), channel_id=1, source_target_pairs={{0,4},{2,6},{4,0},{6,2},{8,12},{10,14},{12,8},{14,10},{16,20},{18,... | collective-permute-start | bytes 3145736 | tf_op jit(solution)/shard_map/ppermute | solution.py:28
  103.9 6.4 %collective-permute-start.8 = (bf16[16,2,16,512]{3,2,1,0:T(8,128)(2,1)}, bf16[16,2,16,512]{3,2,1,0:T(8,128)(2,1)S(1)}, u32[]{:S(2)}, u32[]{:S(2)}) collective-permute-start(bf16[16,2,16,512]{3,2,1,0:T(8,128)(2,1)} %get-tuple-element.119), channel_id=1, source_target_pairs={{0,24},{2,26},{4,28},{6,30},{8,16},{10,18},{12,20},{14,22},{16,8},... | collective-permute-start | bytes 1572872 | tf_op jit(solution)/shard_map/ppermute | solution.py:28
  110.8 12.0 %collective-permute-done.8.refs_0_ = bf16[16,2,16,512]{3,2,1,0:T(8,128)(2,1)S(1)} collective-permute-done((bf16[16,2,16,512]{3,2,1,0:T(8,128)(2,1)}, bf16[16,2,16,512]{3,2,1,0:T(8,128)(2,1)S(1)}, u32[]{:S(2)}, u32[]{:S(2)}) %collective-permute-start.8) | collective-permute-done | bytes 524320 | tf_op jit(solution)/shard_map/ppermute | solution.py:28
  128.1 21.3 %collective-permute-done.11.refs_4_ = bf16[2048,256]{1,0:T(8,128)(2,1)} collective-permute-done((bf16[2048,256]{1,0:T(8,128)(2,1)}, bf16[2048,256]{1,0:T(8,128)(2,1)}, u32[]{:S(2)}, u32[]{:S(2)}) %collective-permute-start.11) | collective-permute-done | bytes 1048608 | tf_op jit(solution)/shard_map/ppermute | solution.py:28
  149.4 4.5 collective-permute-start.17
  177.5 49.5 %collective-permute-start.18 = (bf16[16,2,16,512]{3,2,1,0:T(8,128)(2,1)}, bf16[16,2,16,512]{3,2,1,0:T(8,128)(2,1)S(1)}, u32[]{:S(2)}, u32[]{:S(2)}) collective-permute-start(bf16[16,2,16,512]{3,2,1,0:T(8,128)(2,1)} %get-tuple-element.136), channel_id=1, source_target_pairs={{0,28},{2,30},{4,24},{6,26},{8,20},{10,22},{12,16},{14,18},{16,12}... | collective-permute-start | bytes 1572872 | tf_op jit(solution)/shard_map/ppermute | solution.py:28
  228.0 18.6 %shard_map.96 = (bf16[1024,256]{1,0:T(8,128)(2,1)}, bf16[1024,256]{1,0:T(8,128)(2,1)}, bf16[1024,256]{1,0:T(8,128)(2,1)}, bf16[1024,256]{1,0:T(8,128)(2,1)}, bf1...) custom-call(bf16[256,7680]{1,0:T(8,128)(2,1)} %shard_map.95.refs_0_, ...), custom_call_target="tpu_custom_call" | custom-call | flops 10737418240 | bytes 8388608 | tf_op jit(solution)/shard_map/pallas_call | solution.py:91
  251.7 4.7 collective-permute-start.24
  256.9 6.2 %collective-permute-done.21.refs_3_ = bf16[1024,256]{1,0:T(8,128)(2,1)S(1)} collective-permute-done((bf16[1024,256]{1,0:T(8,128)(2,1)}, bf16[1024,256]{1,0:T(8,128)(2,1)S(1)}, u32[]{:S(2)}, u32[]{:S(2)}) %collective-permute-start.21) | collective-permute-done | bytes 524320 | tf_op jit(solution)/shard_map/ppermute | solution.py:28
  266.7 7.4 %collective-permute-done.22.refs_4_ = bf16[1024,256]{1,0:T(8,128)(2,1)S(1)} collective-permute-done((bf16[1024,256]{1,0:T(8,128)(2,1)}, bf16[1024,256]{1,0:T(8,128)(2,1)S(1)}, u32[]{:S(2)}, u32[]{:S(2)}) %collective-permute-start.22) | collective-permute-done | bytes 524320 | tf_op jit(solution)/shard_map/ppermute | solution.py:28
  280.0 23.3 %collective-permute-done.24.refs_0_ = bf16[16,2,64,256]{3,2,1,0:T(8,128)(2,1)S(1)} collective-permute-done((bf16[16,2,64,256]{3,2,1,0:T(8,128)(2,1)}, bf16[16,2,64,256]{3,2,1,0:T(8,128)(2,1)S(1)}, u32[]{:S(2)}, u32[]{:S(2)}) %collective-permute-start.24) | collective-permute-done | bytes 1048608 | tf_op jit(solution)/shard_map/ppermute | solution.py:28
  304.8 29.6 %collective-permute-done.26.refs_0_ = bf16[16,2,64,256]{3,2,1,0:T(8,128)(2,1)S(1)} collective-permute-done((bf16[16,2,64,256]{3,2,1,0:T(8,128)(2,1)}, bf16[16,2,64,256]{3,2,1,0:T(8,128)(2,1)S(1)}, u32[]{:S(2)}, u32[]{:S(2)}) %collective-permute-start.26) | collective-permute-done | bytes 1048608 | tf_op jit(solution)/shard_map/ppermute | solution.py:28
  340.6 21.1 %collective-permute-done.34.refs_7_.refs_28_ = bf16[16,2,64,256]{3,2,1,0:T(8,128)(2,1)S(1)} collective-permute-done((bf16[16,2,64,256]{3,2,1,0:T(8,128)(2,1)}, bf16[16,2,64,256]{3,2,1,0:T(8,128)(2,1)S(1)}, u32[]{:S(2)}, u32[]{:S(2)}) %collective-permute-start.34) | collective-permute-done | bytes 1048608 | tf_op jit(solution)/shard_map/ppermute | solution.py:28
  370.4 23.7 %collective-permute-done.30.refs_0_ = bf16[8,2,64,256]{3,2,1,0:T(8,128)(2,1)S(1)} collective-permute-done((bf16[8,2,64,256]{3,2,1,0:T(8,128)(2,1)}, bf16[8,2,64,256]{3,2,1,0:T(8,128)(2,1)S(1)}, u32[]{:S(2)}, u32[]{:S(2)}) %collective-permute-start.30) | collective-permute-done | bytes 524320 | tf_op jit(solution)/shard_map/ppermute | solution.py:28
  398.2 12.2 %collective-permute-done.39.refs_3_.refs_31_ = bf16[8,2,64,256]{3,2,1,0:T(8,128)(2,1)S(1)} collective-permute-done((bf16[8,2,64,256]{3,2,1,0:T(8,128)(2,1)}, bf16[8,2,64,256]{3,2,1,0:T(8,128)(2,1)S(1)}, u32[]{:S(2)}, u32[]{:S(2)}) %collective-permute-start.39) | collective-permute-done | bytes 524320 | tf_op jit(solution)/shard_map/ppermute | solution.py:28
  414.8 6.9 %collective-permute-start.43 = (bf16[8,2,64,256]{3,2,1,0:T(8,128)(2,1)}, bf16[8,2,64,256]{3,2,1,0:T(8,128)(2,1)S(1)}, u32[]{:S(2)}, u32[]{:S(2)}) collective-permute-start(bf16[8,2,64,256]{3,2,1,0:T(8,128)(2,1)} %get-tuple-element.191), channel_id=1, source_target_pairs={{0,8},{2,10},{4,12},{6,14},{8,0},{10,2},{12,4},{14,6},{16,24},{18,... | collective-permute-start | bytes 1572872 | tf_op jit(solution)/shard_map/ppermute | solution.py:28
  434.6 15.5 %collective-permute-done.43.refs_0_ = bf16[8,2,64,256]{3,2,1,0:T(8,128)(2,1)S(1)} collective-permute-done((bf16[8,2,64,256]{3,2,1,0:T(8,128)(2,1)}, bf16[8,2,64,256]{3,2,1,0:T(8,128)(2,1)S(1)}, u32[]{:S(2)}, u32[]{:S(2)}) %collective-permute-start.43) | collective-permute-done | bytes 524320 | tf_op jit(solution)/shard_map/ppermute | solution.py:28
  455.3 22.2 %shard_map.112 = (f32[16,2,512,1024]{3,2,1,0:T(8,128)}, f32[8,128]{1,0:T(8,128)}) custom-call(s32[3]{0:T(128)} %pad_add_fusion.place_ref, f32[16,48,512]{2,1,0:T(8,128)} %bitcast.15, f32[16,48,512]{2,1,0:T(8,128)} %bitcast.17, bf16[16,2,16,512]{3,2,1,0:T(8,128)(2,1)} %get-tuple-element.105.refs_2_, ...), custom_call_target="tpu_custom_call" | custom-call | flops 12884901888 | bytes 33554432 | tf_op jit(solution)/shard_map/pallas_call | solution.py:212
  478.5 22.4 %shard_map.113 = (f32[16,2,512,1024]{3,2,1,0:T(8,128)}, f32[8,128]{1,0:T(8,128)}) custom-call(s32[3]{0:T(128)} %pad_add_fusion.place_ref, f32[16,48,512]{2,1,0:T(8,128)} %bitcast.16, f32[16,48,512]{2,1,0:T(8,128)} %bitcast.18, bf16[16,2,16,512]{3,2,1,0:T(8,128)(2,1)} %get-tuple-element.105.refs_2_, ...), custom_call_target="tpu_custom_call", output_to_operand_aliasing={{0}: (35, {})} | custom-call | flops 12884901888 | bytes 33554432 | tf_op jit(solution)/shard_map/pallas_call | solution.py:212
  (230 shorter events, 124.3 us)
Async XLA Ops:
  5.8 66.9 %collective-permute-start.6 = (bf16[256,7680]{1,0:T(8,128)(2,1)}, bf16[256,7680]{1,0:T(8,128)(2,1)}, u32[]{:S(2)}, u32[]{:S(2)}) collective-permute-start(bf16[256,7680]{1,0:T(8,128)(2,1)} %get-tuple-element.200), channel_id=1, source_target_pairs={{0,2},{2,4},{4,6},{6,8},{8,10},{10,12},{12,14},{14,16},{16,18},{18... | collective-permute-start | bytes 11796488 | tf_op jit(solution)/shard_map/ppermute | solution.py:24
  44.2 27.1 %collective-permute-start.4 = (bf16[16,2,16,512]{3,2,1,0:T(8,128)(2,1)}, bf16[16,2,16,512]{3,2,1,0:T(8,128)(2,1)S(1)}, u32[]{:S(2)}, u32[]{:S(2)}) collective-permute-start(bf16[16,2,16,512]{3,2,1,0:T(8,128)(2,1)} %get-tuple-element.105.refs_2_), channel_id=1, source_target_pairs={{0,1},{1,0},{2,3},{3,2},{4,5},{5,4},{6,7},{7,6},{8,9},{9,8},{10,11... | collective-permute-start | bytes 1572872 | tf_op jit(solution)/shard_map/ppermute | solution.py:28
  55.2 36.2 %collective-permute-start.5 = (bf16[16,2,16,512]{3,2,1,0:T(8,128)(2,1)S(1)}, bf16[16,2,16,512]{3,2,1,0:T(8,128)(2,1)S(1)}, u32[]{:S(2)}, u32[]{:S(2)}) collective-permute-start(bf16[16,2,16,512]{3,2,1,0:T(8,128)(2,1)S(1)} %copy-done.46), channel_id=1, source_target_pairs={{0,12},{2,14},{4,8},{6,10},{8,4},{10,6},{12,0},{14,2},{16,28},{18,... | collective-permute-start | bytes 1572872 | tf_op jit(solution)/shard_map/ppermute | solution.py:28
  92.4 31.5 %collective-permute-start.9 = (bf16[2048,256]{1,0:T(8,128)(2,1)}, bf16[2048,256]{1,0:T(8,128)(2,1)S(1)}, u32[]{:S(2)}, u32[]{:S(2)}) collective-permute-start(bf16[2048,256]{1,0:T(8,128)(2,1)} %get-tuple-element.121), channel_id=1, source_target_pairs={{0,2},{2,0},{4,6},{6,4},{8,10},{10,8},{12,14},{14,12},{16,18},{18,... | collective-permute-start | bytes 3145736 | tf_op jit(solution)/shard_map/ppermute | solution.py:28
  92.4 35.7 %collective-permute-start.10 = (bf16[2048,256]{1,0:T(8,128)(2,1)}, bf16[2048,256]{1,0:T(8,128)(2,1)S(1)}, u32[]{:S(2)}, u32[]{:S(2)}) collective-permute-start(bf16[2048,256]{1,0:T(8,128)(2,1)} %get-tuple-element.122), channel_id=1, source_target_pairs={{0,4},{2,6},{4,0},{6,2},{8,12},{10,14},{12,8},{14,10},{16,20},{18,... | collective-permute-start | bytes 3145736 | tf_op jit(solution)/shard_map/ppermute | solution.py:28
  103.9 45.5 %collective-permute-start.11 = (bf16[2048,256]{1,0:T(8,128)(2,1)}, bf16[2048,256]{1,0:T(8,128)(2,1)}, u32[]{:S(2)}, u32[]{:S(2)}) collective-permute-start(bf16[2048,256]{1,0:T(8,128)(2,1)} %get-tuple-element.123), channel_id=1, source_target_pairs={{0,6},{2,4},{4,2},{6,0},{8,14},{10,12},{12,10},{14,8},{16,22},{18,... | collective-permute-start | bytes 3145736 | tf_op jit(solution)/shard_map/ppermute | solution.py:28
  149.4 77.6 %collective-permute-start.17 = (bf16[256,7680]{1,0:T(8,128)(2,1)}, bf16[256,7680]{1,0:T(8,128)(2,1)}, u32[]{:S(2)}, u32[]{:S(2)}) collective-permute-start(bf16[256,7680]{1,0:T(8,128)(2,1)} %shard_map.93), channel_id=1, source_target_pairs={{0,2},{2,4},{4,6},{6,8},{8,10},{10,12},{12,14},{14,16},{16,18},{18... | collective-permute-start | bytes 11796488 | tf_op jit(solution)/shard_map/ppermute | solution.py:24
  155.4 71.6 %collective-permute-start.15 = (bf16[16,2,16,512]{3,2,1,0:T(8,128)(2,1)}, bf16[16,2,16,512]{3,2,1,0:T(8,128)(2,1)S(1)}, u32[]{:S(2)}, u32[]{:S(2)}) collective-permute-start(bf16[16,2,16,512]{3,2,1,0:T(8,128)(2,1)} %get-tuple-element.133), channel_id=1, source_target_pairs={{0,20},{2,22},{4,16},{6,18},{8,28},{10,30},{12,24},{14,26},{16,4},... | collective-permute-start | bytes 1572872 | tf_op jit(solution)/shard_map/ppermute | solution.py:28
  158.8 68.1 %collective-permute-start.16 = (bf16[16,2,16,512]{3,2,1,0:T(8,128)(2,1)S(1)}, bf16[16,2,16,512]{3,2,1,0:T(8,128)(2,1)S(1)}, u32[]{:S(2)}, u32[]{:S(2)}) collective-permute-start(bf16[16,2,16,512]{3,2,1,0:T(8,128)(2,1)S(1)} %copy-done.5), channel_id=1, source_target_pairs={{0,1},{1,0},{2,3},{3,2},{4,5},{5,4},{6,7},{7,6},{8,9},{9,8},{10,11... | collective-permute-start | bytes 1572872 | tf_op jit(solution)/shard_map/ppermute | solution.py:28
  177.0 69.7 %collective-permute-start.19 = (bf16[16,2,16,512]{3,2,1,0:T(8,128)(2,1)}, bf16[16,2,16,512]{3,2,1,0:T(8,128)(2,1)S(1)}, u32[]{:S(2)}, u32[]{:S(2)}) collective-permute-start(bf16[16,2,16,512]{3,2,1,0:T(8,128)(2,1)} %get-tuple-element.132.refs_2_.refs_1_.refs_7_), channel_id=1, source_target_pairs={{0,1},{1,0},{2,3},{3,2},{4,5},{5,4},{6,7},{7,6},{8,9},{9,8},{10,11... | collective-permute-start | bytes 1572872 | tf_op jit(solution)/shard_map/ppermute | solution.py:28
  177.5 69.2 %collective-permute-start.18 = (bf16[16,2,16,512]{3,2,1,0:T(8,128)(2,1)}, bf16[16,2,16,512]{3,2,1,0:T(8,128)(2,1)S(1)}, u32[]{:S(2)}, u32[]{:S(2)}) collective-permute-start(bf16[16,2,16,512]{3,2,1,0:T(8,128)(2,1)} %get-tuple-element.136), channel_id=1, source_target_pairs={{0,28},{2,30},{4,24},{6,26},{8,20},{10,22},{12,16},{14,18},{16,12}... | collective-permute-start | bytes 1572872 | tf_op jit(solution)/shard_map/ppermute | solution.py:28
  251.7 51.7 %collective-permute-start.24 = (bf16[16,2,64,256]{3,2,1,0:T(8,128)(2,1)}, bf16[16,2,64,256]{3,2,1,0:T(8,128)(2,1)S(1)}, u32[]{:S(2)}, u32[]{:S(2)}) collective-permute-start(bf16[16,2,64,256]{3,2,1,0:T(8,128)(2,1)} %get-tuple-element.150), channel_id=1, source_target_pairs={{0,16},{2,18},{4,20},{6,22},{8,24},{10,26},{12,28},{14,30},{16,0},... | collective-permute-start | bytes 3145736 | tf_op jit(solution)/shard_map/ppermute | solution.py:28
  264.0 70.5 %collective-permute-start.26 = (bf16[16,2,64,256]{3,2,1,0:T(8,128)(2,1)}, bf16[16,2,64,256]{3,2,1,0:T(8,128)(2,1)S(1)}, u32[]{:S(2)}, u32[]{:S(2)}) collective-permute-start(bf16[16,2,64,256]{3,2,1,0:T(8,128)(2,1)} %get-tuple-element.157), channel_id=1, source_target_pairs={{0,8},{2,10},{4,12},{6,14},{8,0},{10,2},{12,4},{14,6},{16,24},{18,... | collective-permute-start | bytes 3145736 | tf_op jit(solution)/shard_map/ppermute | solution.py:28
  275.7 58.7 %collective-permute-start.27 = (bf16[16,2,64,256]{3,2,1,0:T(8,128)(2,1)}, bf16[16,2,64,256]{3,2,1,0:T(8,128)(2,1)}, u32[]{:S(2)}, u32[]{:S(2)}) collective-permute-start(bf16[16,2,64,256]{3,2,1,0:T(8,128)(2,1)} %get-tuple-element.149.refs_2_.refs_10_), channel_id=1, source_target_pairs={{0,1},{1,0},{2,3},{3,2},{4,5},{5,4},{6,7},{7,6},{8,9},{9,8},{10,11... | collective-permute-start | bytes 3145736 | tf_op jit(solution)/shard_map/ppermute | solution.py:28
  277.2 59.7 %collective-permute-start.28 = (bf16[16,2,64,256]{3,2,1,0:T(8,128)(2,1)}, bf16[16,2,64,256]{3,2,1,0:T(8,128)(2,1)S(1)}, u32[]{:S(2)}, u32[]{:S(2)}) collective-permute-start(bf16[16,2,64,256]{3,2,1,0:T(8,128)(2,1)} %get-tuple-element.160), channel_id=1, source_target_pairs={{0,24},{2,26},{4,28},{6,30},{8,16},{10,18},{12,20},{14,22},{16,8},... | collective-permute-start | bytes 3145736 | tf_op jit(solution)/shard_map/ppermute | solution.py:28
  304.3 32.6 %collective-permute-start.29 = (bf16[16,2,64,256]{3,2,1,0:T(8,128)(2,1)}, bf16[16,2,64,256]{3,2,1,0:T(8,128)(2,1)S(1)}, u32[]{:S(2)}, u32[]{:S(2)}) collective-permute-start(bf16[16,2,64,256]{3,2,1,0:T(8,128)(2,1)} %get-tuple-element.156.refs_2_.refs_11_), channel_id=1, source_target_pairs={{0,1},{1,0},{2,3},{3,2},{4,5},{5,4},{6,7},{7,6},{8,9},{9,8},{10,11... | collective-permute-start | bytes 3145736 | tf_op jit(solution)/shard_map/ppermute | solution.py:28
  338.2 55.9 %collective-permute-start.35 = (bf16[16,2,64,256]{3,2,1,0:T(8,128)(2,1)}, bf16[16,2,64,256]{3,2,1,0:T(8,128)(2,1)S(1)}, u32[]{:S(2)}, u32[]{:S(2)}) collective-permute-start(bf16[16,2,64,256]{3,2,1,0:T(8,128)(2,1)} %get-tuple-element.166.refs_6_.refs_13_), channel_id=1, source_target_pairs={{0,1},{1,0},{2,3},{3,2},{4,5},{5,4},{6,7},{7,6},{8,9},{9,8},{10,11... | collective-permute-start | bytes 3145736 | tf_op jit(solution)/shard_map/ppermute | solution.py:28
  361.7 32.4 %collective-permute-start.30 = (bf16[8,2,64,256]{3,2,1,0:T(8,128)(2,1)}, bf16[8,2,64,256]{3,2,1,0:T(8,128)(2,1)S(1)}, u32[]{:S(2)}, u32[]{:S(2)}) collective-permute-start(bf16[8,2,64,256]{3,2,1,0:T(8,128)(2,1)} %get-tuple-element.167), channel_id=1, source_target_pairs={{0,16},{2,18},{4,20},{6,22},{8,24},{10,26},{12,28},{14,30},{16,0},... | collective-permute-start | bytes 1572872 | tf_op jit(solution)/shard_map/ppermute | solution.py:28
  361.7 35.1 %collective-permute-start.37 = (bf16[8,2,64,256]{3,2,1,0:T(8,128)(2,1)}, bf16[8,2,64,256]{3,2,1,0:T(8,128)(2,1)}, u32[]{:S(2)}, u32[]{:S(2)}) collective-permute-start(bf16[8,2,64,256]{3,2,1,0:T(8,128)(2,1)} %get-tuple-element.184), channel_id=1, source_target_pairs={{0,8},{2,10},{4,12},{6,14},{8,0},{10,2},{12,4},{14,6},{16,24},{18,... | collective-permute-start | bytes 1572872 | tf_op jit(solution)/shard_map/ppermute | solution.py:28
  364.3 33.9 %collective-permute-start.36 = (bf16[8,2,64,256]{3,2,1,0:T(8,128)(2,1)}, bf16[8,2,64,256]{3,2,1,0:T(8,128)(2,1)S(1)}, u32[]{:S(2)}, u32[]{:S(2)}) collective-permute-start(bf16[8,2,64,256]{3,2,1,0:T(8,128)(2,1)} %get-tuple-element.182), channel_id=1, source_target_pairs={{0,24},{2,26},{4,28},{6,30},{8,16},{10,18},{12,20},{14,22},{16,8},... | collective-permute-start | bytes 1572872 | tf_op jit(solution)/shard_map/ppermute | solution.py:28
  366.2 30.7 %collective-permute-start.38 = (bf16[8,2,64,256]{3,2,1,0:T(8,128)(2,1)}, bf16[8,2,64,256]{3,2,1,0:T(8,128)(2,1)S(1)}, u32[]{:S(2)}, u32[]{:S(2)}) collective-permute-start(bf16[8,2,64,256]{3,2,1,0:T(8,128)(2,1)} %get-tuple-element.179.refs_2_.refs_14_), channel_id=1, source_target_pairs={{0,1},{1,0},{2,3},{3,2},{4,5},{5,4},{6,7},{7,6},{8,9},{9,8},{10,11... | collective-permute-start | bytes 1572872 | tf_op jit(solution)/shard_map/ppermute | solution.py:28
  398.2 29.6 %collective-permute-start.41 = (bf16[8,2,64,256]{3,2,1,0:T(8,128)(2,1)}, bf16[8,2,64,256]{3,2,1,0:T(8,128)(2,1)S(1)}, u32[]{:S(2)}, u32[]{:S(2)}) collective-permute-start(bf16[8,2,64,256]{3,2,1,0:T(8,128)(2,1)} %get-tuple-element.190), channel_id=1, source_target_pairs={{0,16},{2,18},{4,20},{6,22},{8,24},{10,26},{12,28},{14,30},{16,0},... | collective-permute-start | bytes 1572872 | tf_op jit(solution)/shard_map/ppermute | solution.py:28
  414.8 35.2 %collective-permute-start.43 = (bf16[8,2,64,256]{3,2,1,0:T(8,128)(2,1)}, bf16[8,2,64,256]{3,2,1,0:T(8,128)(2,1)S(1)}, u32[]{:S(2)}, u32[]{:S(2)}) collective-permute-start(bf16[8,2,64,256]{3,2,1,0:T(8,128)(2,1)} %get-tuple-element.191), channel_id=1, source_target_pairs={{0,8},{2,10},{4,12},{6,14},{8,0},{10,2},{12,4},{14,6},{16,24},{18,... | collective-permute-start | bytes 1572872 | tf_op jit(solution)/shard_map/ppermute | solution.py:28
  422.5 30.7 %collective-permute-start.45 = (bf16[8,2,64,256]{3,2,1,0:T(8,128)(2,1)}, bf16[8,2,64,256]{3,2,1,0:T(8,128)(2,1)S(1)}, u32[]{:S(2)}, u32[]{:S(2)}) collective-permute-start(bf16[8,2,64,256]{3,2,1,0:T(8,128)(2,1)} %get-tuple-element.192), channel_id=1, source_target_pairs={{0,24},{2,26},{4,28},{6,30},{8,16},{10,18},{12,20},{14,22},{16,8},... | collective-permute-start | bytes 1572872 | tf_op jit(solution)/shard_map/ppermute | solution.py:28
  (74 other events, 763.3 us)

commit v3 on v2

--- a/solution.py
+++ b/solution.py
@@ -147,7 +147,7 @@
 
 
 def correlate_kernel(layout, scale, place_ref, *refs):
-    (out_ref, token_ref), (lhs_re, lhs_im, rhs) = refs[-5:-3], refs[-3:]
+    (out_ref, token_ref), (lhs, rhs) = refs[-4:-2], refs[-2:]
     token_ref[...] = jnp.zeros_like(token_ref)
     total = rhs.shape[0] // 2
     sides, width, frames = layout["sides"], layout["width"], layout["frames"]
@@ -174,12 +174,13 @@
                     ).astype(BF16)
             if side == 0:
                 turned = rhs[...].T
-                lhs_re[...] = turned
-                lhs_im[:, :total] = turned[:, total:]
-                lhs_im[:, total:] = -turned[:, :total]
+                lhs[:width, :] = turned
+                lhs[width:, :total] = turned[:, total:]
+                lhs[width:, total:] = -turned[:, :total]
             columns = pl.ds(pl.multiple_of(place_ref[side] * LANES, LANES), width)
-            for r, lhs in enumerate((lhs_re, lhs_im)):
-                out_ref[c, r, :, columns] = scale * jnp.dot(lhs[...], rhs[...], preferred_element_type=F32)
+            both = scale * jnp.dot(lhs[...], rhs[...], preferred_element_type=F32)
+            for r in range(2):
+                out_ref[c, r, :, columns] = both[r * width : (r + 1) * width]
 
 
 def correlated(result, first, chans, local, others, keeps, place, shape, scale, frames, devices):
@@ -220,8 +221,7 @@
                 pl.BlockSpec((STEP, LANES), lambda c, place: (0, 0)),
             ],
             scratch_shapes=[
-                pltpu.VMEM((signals, 2 * total), BF16),
-                pltpu.VMEM((signals, 2 * total), BF16),
+                pltpu.VMEM((2 * signals, 2 * total), BF16),
                 pltpu.VMEM((2 * total, signals), BF16),
             ],
         ),
@@ -402,10 +402,10 @@
 SENDS = {8: (0, 2, 4, 3, 6, 1, 5, 7), 4: (0, 2, 1, 3)}
 AHEAD = 3
 DEPTH = 2
-LEAD = 3
+LEAD = 4
 NEARS = (2, 4, 4, 4)
 SPLITS = (1, 1)
-FIRST_PIECE = 4
+FIRST_PIECE = 3
 PIECES = 1
 LATER = 3
 

time: 502 us -> 501 us (level)
  starting transfers between devices: 137 us -> 203 us
  waiting for transfers between devices: 197 us -> 134 us
    ppermute x47, starting transfers between devices: 128 us -> 195 us  [swapped(): lax.ppermute(block, axis, [(i, i ^ mask) for i in range(lax.axis_size(axi...]
    ppermute x47, waiting for transfers between devices: 197 us -> 134 us  [swapped(): lax.ppermute(block, axis, [(i, i ^ mask) for i in range(lax.axis_size(axi...]
  transfers between devices with their start and end apart: 49 -> 49, of which waited for: 19 -> 18; matrix products, arithmetic and copies ran while one was open for 5% -> 4% of each run, Pallas kernels for 18% -> 19%
where the time goes in v3:
time: 501 us; the launch traced here: 498 us
  starting transfers between devices  203 us (41%)
  waiting for transfers between devices  134 us (27%)
  Pallas kernels  115 us (23%)
  local copies, waits for them, and re-layouts  38 us (8%)
    ppermute x47, starting transfers between devices, swapped(): lax.ppermute(block, axis, [(i, i ^ mask) for i in range(lax.axis_size(axi...  195 us
    ppermute x47, waiting for transfers between devices, swapped(): lax.ppermute(block, axis, [(i, i ^ mask) for i in range(lax.axis_size(axi...  134 us
    pallas_call x3, Pallas kernels, spectra(): pl.pallas_call(functools.partial(spectra_kernel, start, count, len(halos)...  55.6 us
    pallas_call x2, Pallas kernels, correlated(): pl.pallas_call(functools.partial(correlate_kernel, layout, scale), grid_s...  45 us
    unnamed x98, local copies, waits for them, and re-layouts  21.1 us
    pallas_call x4, Pallas kernels, joined(): pl.pallas_call(functools.partial(join_kernel, count, pieces), grid=(signa...  14.4 us
  transfers between devices with their start and end apart: 49, of which 18 were waited for; matrix products, arithmetic and copies ran while one was open for 4% of the time, Pallas kernels for 19%

profile of v3, /device:TPU:0, one launch (start us, length us, event | category | flops | bytes accessed | tf_op | source)
XLA Modules:
  0.0 497.9 jit_solution(12890923948498539010)
XLA Ops:
  0.0 5.8 %fusion.1 = (bf16[256,7680]{1,0:T(8,128)(2,1)}, bf16[256,7680]{1,0:T(8,128)(2,1)}) fusion(bf16[512,12288]{1,0:T(8,128)(2,1)} %refs_1_.5), kind=kLoop, calls=%fused_computation.19 | loop fusion | bytes 15728640 | tf_op jit(solution)/shard_map/slice | solution.py:272
  13.3 18.2 %shard_map.82 = (bf16[2048,512]{1,0:T(8,128)(2,1)}, bf16[2048,512]{1,0:T(8,128)(2,1)}) custom-call(bf16[512,12288]{1,0:T(8,128)(2,1)} %refs_1_.5, f32[16,512]{1,0:T(8,128)} %refs_2_.3, bf16[512,512]{1,0:T(8,128)(2,1)} %reshape.32.refs_2_), custom_call_target="tpu_custom_call" | custom-call | flops 10737418240 | bytes 16777216 | tf_op jit(solution)/shard_map/pallas_call | solution.py:91
  37.6 5.0 %shard_map.83 = (bf16[16,2,16,512]{3,2,1,0:T(8,128)(2,1)}, bf16[16,2,16,512]{3,2,1,0:T(8,128)(2,1)}, bf16[16,2,16,512]{3,2,1,0:T(8,128)(2,1)}, bf16[16,2,16,512]...) custom-call(bf16[2048,512]{1,0:T(8,128)(2,1)} %get-tuple-element.101, ...), custom_call_target="tpu_custom_call" | custom-call | flops 2097152 | bytes 8388608 | tf_op jit(solution)/shard_map/pallas_call | solution.py:130
  57.8 9.7 %collective-permute-done.2.refs_0_ = bf16[16,2,16,512]{3,2,1,0:T(8,128)(2,1)S(1)} collective-permute-done((bf16[16,2,16,512]{3,2,1,0:T(8,128)(2,1)}, bf16[16,2,16,512]{3,2,1,0:T(8,128)(2,1)S(1)}, u32[]{:S(2)}, u32[]{:S(2)}) %collective-permute-start.2) | collective-permute-done | bytes 524320 | tf_op jit(solution)/shard_map/ppermute | solution.py:28
  72.6 18.7 %shard_map.88 = (bf16[2048,256]{1,0:T(8,128)(2,1)}, bf16[2048,256]{1,0:T(8,128)(2,1)}, bf16[2048,256]{1,0:T(8,128)(2,1)}, bf16[2048,256]{1,0:T(8,128)(2,1)}) custom-call(bf16[256,7680]{1,0:T(8,128)(2,1)} %shard_map.87.refs_0_, bf16[512,12288]{1,0:T(8,128)(2,1)} %refs_1_.5, f32[16,512]{1,0:T(8,128)} %refs_2_.3, bf16[512,512]{1,0:T(8,128)(2,1)} %reshape.33.refs_3_), custom_call_target="tpu_custom_call" | custom-call | flops 10737418240 | bytes 8388608 | tf_op jit(solution)/shard_map/pallas_call | solution.py:91
  95.8 5.7 %collective-permute-start.8 = (bf16[16,2,16,512]{3,2,1,0:T(8,128)(2,1)S(1)}, bf16[16,2,16,512]{3,2,1,0:T(8,128)(2,1)S(1)}, u32[]{:S(2)}, u32[]{:S(2)}) collective-permute-start(bf16[16,2,16,512]{3,2,1,0:T(8,128)(2,1)S(1)} %copy-done.41), channel_id=1, source_target_pairs={{0,24},{2,26},{4,28},{6,30},{8,16},{10,18},{12,20},{14,22},{16,8},... | collective-permute-start | bytes 1572872 | tf_op jit(solution)/shard_map/ppermute | solution.py:28
  101.6 11.0 %collective-permute-start.10 = (bf16[2048,256]{1,0:T(8,128)(2,1)}, bf16[2048,256]{1,0:T(8,128)(2,1)S(1)}, u32[]{:S(2)}, u32[]{:S(2)}) collective-permute-start(bf16[2048,256]{1,0:T(8,128)(2,1)} %get-tuple-element.122), channel_id=1, source_target_pairs={{0,4},{2,6},{4,0},{6,2},{8,12},{10,14},{12,8},{14,10},{16,20},{18,... | collective-permute-start | bytes 3145736 | tf_op jit(solution)/shard_map/ppermute | solution.py:28
  113.3 13.4 %collective-permute-done.12.refs_7_.refs_20_ = bf16[16,2,16,512]{3,2,1,0:T(8,128)(2,1)S(1)} collective-permute-done((bf16[16,2,16,512]{3,2,1,0:T(8,128)(2,1)S(1)}, bf16[16,2,16,512]{3,2,1,0:T(8,128)(2,1)S(1)}, u32[]{:S(2)}, u32[]{:S(2)}) %collective-permute-start.12) | collective-permute-done | bytes 524320 | tf_op jit(solution)/shard_map/ppermute | solution.py:28
  127.5 7.4 %collective-permute-start.13 = (bf16[16,2,16,512]{3,2,1,0:T(8,128)(2,1)}, bf16[16,2,16,512]{3,2,1,0:T(8,128)(2,1)S(1)}, u32[]{:S(2)}, u32[]{:S(2)}) collective-permute-start(bf16[16,2,16,512]{3,2,1,0:T(8,128)(2,1)} %get-tuple-element.126), channel_id=1, source_target_pairs={{0,4},{2,6},{4,0},{6,2},{8,12},{10,14},{12,8},{14,10},{16,20},{18,... | collective-permute-start | bytes 1572872 | tf_op jit(solution)/shard_map/ppermute | solution.py:28
  137.8 30.5 %collective-permute-start.16 = (bf16[16,2,16,512]{3,2,1,0:T(8,128)(2,1)}, bf16[16,2,16,512]{3,2,1,0:T(8,128)(2,1)S(1)}, u32[]{:S(2)}, u32[]{:S(2)}) collective-permute-start(bf16[16,2,16,512]{3,2,1,0:T(8,128)(2,1)} %get-tuple-element.133), channel_id=1, source_target_pairs={{0,20},{2,22},{4,16},{6,18},{8,28},{10,30},{12,24},{14,26},{16,4},... | collective-permute-start | bytes 1572872 | tf_op jit(solution)/shard_map/ppermute | solution.py:28
  177.6 43.7 %collective-permute-start.18 = (bf16[16,2,16,512]{3,2,1,0:T(8,128)(2,1)}, bf16[16,2,16,512]{3,2,1,0:T(8,128)(2,1)S(1)}, u32[]{:S(2)}, u32[]{:S(2)}) collective-permute-start(bf16[16,2,16,512]{3,2,1,0:T(8,128)(2,1)} %get-tuple-element.136), channel_id=1, source_target_pairs={{0,28},{2,30},{4,24},{6,26},{8,20},{10,22},{12,16},{14,18},{16,12}... | collective-permute-start | bytes 1572872 | tf_op jit(solution)/shard_map/ppermute | solution.py:28
  224.5 18.6 %shard_map.96 = (bf16[1024,256]{1,0:T(8,128)(2,1)}, bf16[1024,256]{1,0:T(8,128)(2,1)}, bf16[1024,256]{1,0:T(8,128)(2,1)}, bf16[1024,256]{1,0:T(8,128)(2,1)}, bf1...) custom-call(bf16[256,7680]{1,0:T(8,128)(2,1)} %shard_map.95.refs_0_, ...), custom_call_target="tpu_custom_call" | custom-call | flops 10737418240 | bytes 8388608 | tf_op jit(solution)/shard_map/pallas_call | solution.py:91
  247.5 24.1 %collective-permute-start.26 = (bf16[16,2,64,256]{3,2,1,0:T(8,128)(2,1)}, bf16[16,2,64,256]{3,2,1,0:T(8,128)(2,1)S(1)}, u32[]{:S(2)}, u32[]{:S(2)}) collective-permute-start(bf16[16,2,64,256]{3,2,1,0:T(8,128)(2,1)} %get-tuple-element.157), channel_id=1, source_target_pairs={{0,8},{2,10},{4,12},{6,14},{8,0},{10,2},{12,4},{14,6},{16,24},{18,... | collective-permute-start | bytes 3145736 | tf_op jit(solution)/shard_map/ppermute | solution.py:28
  276.2 10.8 %collective-permute-done.24.refs_0_ = bf16[16,2,64,256]{3,2,1,0:T(8,128)(2,1)S(1)} collective-permute-done((bf16[16,2,64,256]{3,2,1,0:T(8,128)(2,1)}, bf16[16,2,64,256]{3,2,1,0:T(8,128)(2,1)S(1)}, u32[]{:S(2)}, u32[]{:S(2)}) %collective-permute-start.24) | collective-permute-done | bytes 1048608 | tf_op jit(solution)/shard_map/ppermute | solution.py:28
  289.4 42.4 %collective-permute-done.26.refs_0_ = bf16[16,2,64,256]{3,2,1,0:T(8,128)(2,1)S(1)} collective-permute-done((bf16[16,2,64,256]{3,2,1,0:T(8,128)(2,1)}, bf16[16,2,64,256]{3,2,1,0:T(8,128)(2,1)S(1)}, u32[]{:S(2)}, u32[]{:S(2)}) %collective-permute-start.26) | collective-permute-done | bytes 1048608 | tf_op jit(solution)/shard_map/ppermute | solution.py:28
  338.5 9.4 %collective-permute-start.30 = (bf16[8,2,64,256]{3,2,1,0:T(8,128)(2,1)}, bf16[8,2,64,256]{3,2,1,0:T(8,128)(2,1)S(1)}, u32[]{:S(2)}, u32[]{:S(2)}) collective-permute-start(bf16[8,2,64,256]{3,2,1,0:T(8,128)(2,1)} %get-tuple-element.167), channel_id=1, source_target_pairs={{0,16},{2,18},{4,20},{6,22},{8,24},{10,26},{12,28},{14,30},{16,0},... | collective-permute-start | bytes 1572872 | tf_op jit(solution)/shard_map/ppermute | solution.py:28
  351.4 8.4 %collective-permute-start.37 = (bf16[8,2,64,256]{3,2,1,0:T(8,128)(2,1)}, bf16[8,2,64,256]{3,2,1,0:T(8,128)(2,1)}, u32[]{:S(2)}, u32[]{:S(2)}) collective-permute-start(bf16[8,2,64,256]{3,2,1,0:T(8,128)(2,1)} %get-tuple-element.184), channel_id=1, source_target_pairs={{0,8},{2,10},{4,12},{6,14},{8,0},{10,2},{12,4},{14,6},{16,24},{18,... | collective-permute-start | bytes 1572872 | tf_op jit(solution)/shard_map/ppermute | solution.py:28
  373.0 8.5 %collective-permute-done.35.refs_3_.refs_29_ = bf16[16,2,64,256]{3,2,1,0:T(8,128)(2,1)S(1)} collective-permute-done((bf16[16,2,64,256]{3,2,1,0:T(8,128)(2,1)}, bf16[16,2,64,256]{3,2,1,0:T(8,128)(2,1)S(1)}, u32[]{:S(2)}, u32[]{:S(2)}) %collective-permute-start.35) | collective-permute-done | bytes 1048608 | tf_op jit(solution)/shard_map/ppermute | solution.py:28
  384.0 8.7 %collective-permute-done.37.refs_0_ = bf16[8,2,64,256]{3,2,1,0:T(8,128)(2,1)} collective-permute-done((bf16[8,2,64,256]{3,2,1,0:T(8,128)(2,1)}, bf16[8,2,64,256]{3,2,1,0:T(8,128)(2,1)}, u32[]{:S(2)}, u32[]{:S(2)}) %collective-permute-start.37) | collective-permute-done | bytes 524320 | tf_op jit(solution)/shard_map/ppermute | solution.py:28
  395.0 7.3 %collective-permute-start.41 = (bf16[8,2,64,256]{3,2,1,0:T(8,128)(2,1)}, bf16[8,2,64,256]{3,2,1,0:T(8,128)(2,1)S(1)}, u32[]{:S(2)}, u32[]{:S(2)}) collective-permute-start(bf16[8,2,64,256]{3,2,1,0:T(8,128)(2,1)} %get-tuple-element.190), channel_id=1, source_target_pairs={{0,16},{2,18},{4,20},{6,22},{8,24},{10,26},{12,28},{14,30},{16,0},... | collective-permute-start | bytes 1572872 | tf_op jit(solution)/shard_map/ppermute | solution.py:28
  408.3 5.9 %collective-permute-start.43 = (bf16[8,2,64,256]{3,2,1,0:T(8,128)(2,1)}, bf16[8,2,64,256]{3,2,1,0:T(8,128)(2,1)S(1)}, u32[]{:S(2)}, u32[]{:S(2)}) collective-permute-start(bf16[8,2,64,256]{3,2,1,0:T(8,128)(2,1)} %get-tuple-element.191), channel_id=1, source_target_pairs={{0,8},{2,10},{4,12},{6,14},{8,0},{10,2},{12,4},{14,6},{16,24},{18,... | collective-permute-start | bytes 1572872 | tf_op jit(solution)/shard_map/ppermute | solution.py:28
  431.2 15.3 %collective-permute-done.43.refs_0_ = bf16[8,2,64,256]{3,2,1,0:T(8,128)(2,1)S(1)} collective-permute-done((bf16[8,2,64,256]{3,2,1,0:T(8,128)(2,1)}, bf16[8,2,64,256]{3,2,1,0:T(8,128)(2,1)S(1)}, u32[]{:S(2)}, u32[]{:S(2)}) %collective-permute-start.43) | collective-permute-done | bytes 524320 | tf_op jit(solution)/shard_map/ppermute | solution.py:28
  451.8 22.4 %shard_map.112 = (f32[16,2,512,1024]{3,2,1,0:T(8,128)}, f32[8,128]{1,0:T(8,128)}) custom-call(s32[3]{0:T(128)} %pad_add_fusion.place_ref, f32[16,48,512]{2,1,0:T(8,128)} %bitcast.15, f32[16,48,512]{2,1,0:T(8,128)} %bitcast.17, bf16[16,2,16,512]{3,2,1,0:T(8,128)(2,1)} %get-tuple-element.105.refs_2_.refs_1_, ...), custom_call_target="tpu_custom_call" | custom-call | flops 12884901888 | bytes 33554432 | tf_op jit(solution)/shard_map/pallas_call | solution.py:213
  475.1 22.6 %shard_map.113 = (f32[16,2,512,1024]{3,2,1,0:T(8,128)}, f32[8,128]{1,0:T(8,128)}) custom-call(s32[3]{0:T(128)} %pad_add_fusion.place_ref, f32[16,48,512]{2,1,0:T(8,128)} %bitcast.16, f32[16,48,512]{2,1,0:T(8,128)} %bitcast.18, bf16[16,2,16,512]{3,2,1,0:T(8,128)(2,1)} %get-tuple-element.105.refs_2_.refs_1_, ...), custom_call_target="tpu_custom_call", output_to_operand_aliasing={{0}: (35, {})} | custom-call | flops 12884901888 | bytes 33554432 | tf_op jit(solution)/shard_map/pallas_call | solution.py:213
  (230 shorter events, 123.8 us)
Async XLA Ops:
  5.8 66.9 %collective-permute-start.6 = (bf16[256,7680]{1,0:T(8,128)(2,1)}, bf16[256,7680]{1,0:T(8,128)(2,1)}, u32[]{:S(2)}, u32[]{:S(2)}) collective-permute-start(bf16[256,7680]{1,0:T(8,128)(2,1)} %get-tuple-element.200), channel_id=1, source_target_pairs={{0,2},{2,4},{4,6},{6,8},{8,10},{10,12},{12,14},{14,16},{16,18},{18... | collective-permute-start | bytes 11796488 | tf_op jit(solution)/shard_map/ppermute | solution.py:24
  55.2 36.2 %collective-permute-start.5 = (bf16[16,2,16,512]{3,2,1,0:T(8,128)(2,1)S(1)}, bf16[16,2,16,512]{3,2,1,0:T(8,128)(2,1)S(1)}, u32[]{:S(2)}, u32[]{:S(2)}) collective-permute-start(bf16[16,2,16,512]{3,2,1,0:T(8,128)(2,1)S(1)} %copy-done.45), channel_id=1, source_target_pairs={{0,12},{2,14},{4,8},{6,10},{8,4},{10,6},{12,0},{14,2},{16,28},{18,... | collective-permute-start | bytes 1572872 | tf_op jit(solution)/shard_map/ppermute | solution.py:28
  92.4 128.9 %collective-permute-start.15 = (bf16[256,7680]{1,0:T(8,128)(2,1)}, bf16[256,7680]{1,0:T(8,128)(2,1)}, u32[]{:S(2)}, u32[]{:S(2)}) collective-permute-start(bf16[256,7680]{1,0:T(8,128)(2,1)} %shard_map.92), channel_id=1, source_target_pairs={{0,2},{2,4},{4,6},{6,8},{8,10},{10,12},{12,14},{14,16},{16,18},{18... | collective-permute-start | bytes 11796488 | tf_op jit(solution)/shard_map/ppermute | solution.py:24
  101.5 33.4 %collective-permute-start.9 = (bf16[2048,256]{1,0:T(8,128)(2,1)}, bf16[2048,256]{1,0:T(8,128)(2,1)S(1)}, u32[]{:S(2)}, u32[]{:S(2)}) collective-permute-start(bf16[2048,256]{1,0:T(8,128)(2,1)} %get-tuple-element.121), channel_id=1, source_target_pairs={{0,2},{2,0},{4,6},{6,4},{8,10},{10,8},{12,14},{14,12},{16,18},{18,... | collective-permute-start | bytes 3145736 | tf_op jit(solution)/shard_map/ppermute | solution.py:28
  101.6 35.2 %collective-permute-start.10 = (bf16[2048,256]{1,0:T(8,128)(2,1)}, bf16[2048,256]{1,0:T(8,128)(2,1)S(1)}, u32[]{:S(2)}, u32[]{:S(2)}) collective-permute-start(bf16[2048,256]{1,0:T(8,128)(2,1)} %get-tuple-element.122), channel_id=1, source_target_pairs={{0,4},{2,6},{4,0},{6,2},{8,12},{10,14},{12,8},{14,10},{16,20},{18,... | collective-permute-start | bytes 3145736 | tf_op jit(solution)/shard_map/ppermute | solution.py:28
  112.5 55.8 %collective-permute-start.11 = (bf16[2048,256]{1,0:T(8,128)(2,1)}, bf16[2048,256]{1,0:T(8,128)(2,1)}, u32[]{:S(2)}, u32[]{:S(2)}) collective-permute-start(bf16[2048,256]{1,0:T(8,128)(2,1)} %get-tuple-element.123), channel_id=1, source_target_pairs={{0,6},{2,4},{4,2},{6,0},{8,14},{10,12},{12,10},{14,8},{16,22},{18,... | collective-permute-start | bytes 3145736 | tf_op jit(solution)/shard_map/ppermute | solution.py:28
  127.5 50.1 %collective-permute-start.13 = (bf16[16,2,16,512]{3,2,1,0:T(8,128)(2,1)}, bf16[16,2,16,512]{3,2,1,0:T(8,128)(2,1)S(1)}, u32[]{:S(2)}, u32[]{:S(2)}) collective-permute-start(bf16[16,2,16,512]{3,2,1,0:T(8,128)(2,1)} %get-tuple-element.126), channel_id=1, source_target_pairs={{0,4},{2,6},{4,0},{6,2},{8,12},{10,14},{12,8},{14,10},{16,20},{18,... | collective-permute-start | bytes 1572872 | tf_op jit(solution)/shard_map/ppermute | solution.py:28
  134.9 86.4 %collective-permute-start.14 = (bf16[16,2,16,512]{3,2,1,0:T(8,128)(2,1)S(1)}, bf16[16,2,16,512]{3,2,1,0:T(8,128)(2,1)}, u32[]{:S(2)}, u32[]{:S(2)}) collective-permute-start(bf16[16,2,16,512]{3,2,1,0:T(8,128)(2,1)S(1)} %copy-done.5), channel_id=1, source_target_pairs={{0,1},{1,0},{2,3},{3,2},{4,5},{5,4},{6,7},{7,6},{8,9},{9,8},{10,11... | collective-permute-start | bytes 1572872 | tf_op jit(solution)/shard_map/ppermute | solution.py:28
  137.8 84.2 %collective-permute-start.16 = (bf16[16,2,16,512]{3,2,1,0:T(8,128)(2,1)}, bf16[16,2,16,512]{3,2,1,0:T(8,128)(2,1)S(1)}, u32[]{:S(2)}, u32[]{:S(2)}) collective-permute-start(bf16[16,2,16,512]{3,2,1,0:T(8,128)(2,1)} %get-tuple-element.133), channel_id=1, source_target_pairs={{0,20},{2,22},{4,16},{6,18},{8,28},{10,30},{12,24},{14,26},{16,4},... | collective-permute-start | bytes 1572872 | tf_op jit(solution)/shard_map/ppermute | solution.py:28
  168.3 53.6 %collective-permute-start.17 = (bf16[16,2,16,512]{3,2,1,0:T(8,128)(2,1)}, bf16[16,2,16,512]{3,2,1,0:T(8,128)(2,1)S(1)}, u32[]{:S(2)}, u32[]{:S(2)}) collective-permute-start(bf16[16,2,16,512]{3,2,1,0:T(8,128)(2,1)} %get-tuple-element.125.refs_2_.refs_1_.refs_6_), channel_id=1, source_target_pairs={{0,1},{1,0},{2,3},{3,2},{4,5},{5,4},{6,7},{7,6},{8,9},{9,8},{10,11... | collective-permute-start | bytes 1572872 | tf_op jit(solution)/shard_map/ppermute | solution.py:28
  177.6 65.5 %collective-permute-start.18 = (bf16[16,2,16,512]{3,2,1,0:T(8,128)(2,1)}, bf16[16,2,16,512]{3,2,1,0:T(8,128)(2,1)S(1)}, u32[]{:S(2)}, u32[]{:S(2)}) collective-permute-start(bf16[16,2,16,512]{3,2,1,0:T(8,128)(2,1)} %get-tuple-element.136), channel_id=1, source_target_pairs={{0,28},{2,30},{4,24},{6,26},{8,20},{10,22},{12,16},{14,18},{16,12}... | collective-permute-start | bytes 1572872 | tf_op jit(solution)/shard_map/ppermute | solution.py:28
  224.5 62.5 %collective-permute-start.24 = (bf16[16,2,64,256]{3,2,1,0:T(8,128)(2,1)}, bf16[16,2,64,256]{3,2,1,0:T(8,128)(2,1)S(1)}, u32[]{:S(2)}, u32[]{:S(2)}) collective-permute-start(bf16[16,2,64,256]{3,2,1,0:T(8,128)(2,1)} %get-tuple-element.150), channel_id=1, source_target_pairs={{0,16},{2,18},{4,20},{6,22},{8,24},{10,26},{12,28},{14,30},{16,0},... | collective-permute-start | bytes 3145736 | tf_op jit(solution)/shard_map/ppermute | solution.py:28
  246.7 40.3 %collective-permute-start.25 = (bf16[16,2,16,512]{3,2,1,0:T(8,128)(2,1)}, bf16[16,2,16,512]{3,2,1,0:T(8,128)(2,1)}, u32[]{:S(2)}, u32[]{:S(2)}) collective-permute-start(bf16[16,2,16,512]{3,2,1,0:T(8,128)(2,1)} %get-tuple-element.142.refs_6_.refs_9_), channel_id=1, source_target_pairs={{0,1},{1,0},{2,3},{3,2},{4,5},{5,4},{6,7},{7,6},{8,9},{9,8},{10,11... | collective-permute-start | bytes 1572872 | tf_op jit(solution)/shard_map/ppermute | solution.py:28
  247.5 84.3 %collective-permute-start.26 = (bf16[16,2,64,256]{3,2,1,0:T(8,128)(2,1)}, bf16[16,2,64,256]{3,2,1,0:T(8,128)(2,1)S(1)}, u32[]{:S(2)}, u32[]{:S(2)}) collective-permute-start(bf16[16,2,64,256]{3,2,1,0:T(8,128)(2,1)} %get-tuple-element.157), channel_id=1, source_target_pairs={{0,8},{2,10},{4,12},{6,14},{8,0},{10,2},{12,4},{14,6},{16,24},{18,... | collective-permute-start | bytes 3145736 | tf_op jit(solution)/shard_map/ppermute | solution.py:28
  272.4 61.9 %collective-permute-start.28 = (bf16[16,2,64,256]{3,2,1,0:T(8,128)(2,1)}, bf16[16,2,64,256]{3,2,1,0:T(8,128)(2,1)S(1)}, u32[]{:S(2)}, u32[]{:S(2)}) collective-permute-start(bf16[16,2,64,256]{3,2,1,0:T(8,128)(2,1)} %get-tuple-element.160), channel_id=1, source_target_pairs={{0,24},{2,26},{4,28},{6,30},{8,16},{10,18},{12,20},{14,22},{16,8},... | collective-permute-start | bytes 3145736 | tf_op jit(solution)/shard_map/ppermute | solution.py:28
  272.6 59.2 %collective-permute-start.27 = (bf16[16,2,64,256]{3,2,1,0:T(8,128)(2,1)}, bf16[16,2,64,256]{3,2,1,0:T(8,128)(2,1)}, u32[]{:S(2)}, u32[]{:S(2)}) collective-permute-start(bf16[16,2,64,256]{3,2,1,0:T(8,128)(2,1)} %get-tuple-element.149.refs_2_.refs_10_), channel_id=1, source_target_pairs={{0,1},{1,0},{2,3},{3,2},{4,5},{5,4},{6,7},{7,6},{8,9},{9,8},{10,11... | collective-permute-start | bytes 3145736 | tf_op jit(solution)/shard_map/ppermute | solution.py:28
  287.9 46.3 %collective-permute-start.29 = (bf16[16,2,64,256]{3,2,1,0:T(8,128)(2,1)}, bf16[16,2,64,256]{3,2,1,0:T(8,128)(2,1)S(1)}, u32[]{:S(2)}, u32[]{:S(2)}) collective-permute-start(bf16[16,2,64,256]{3,2,1,0:T(8,128)(2,1)} %get-tuple-element.156.refs_2_.refs_11_), channel_id=1, source_target_pairs={{0,1},{1,0},{2,3},{3,2},{4,5},{5,4},{6,7},{7,6},{8,9},{9,8},{10,11... | collective-permute-start | bytes 3145736 | tf_op jit(solution)/shard_map/ppermute | solution.py:28
  335.6 45.9 %collective-permute-start.35 = (bf16[16,2,64,256]{3,2,1,0:T(8,128)(2,1)}, bf16[16,2,64,256]{3,2,1,0:T(8,128)(2,1)S(1)}, u32[]{:S(2)}, u32[]{:S(2)}) collective-permute-start(bf16[16,2,64,256]{3,2,1,0:T(8,128)(2,1)} %get-tuple-element.166.refs_6_.refs_13_), channel_id=1, source_target_pairs={{0,1},{1,0},{2,3},{3,2},{4,5},{5,4},{6,7},{7,6},{8,9},{9,8},{10,11... | collective-permute-start | bytes 3145736 | tf_op jit(solution)/shard_map/ppermute | solution.py:28
  338.5 34.5 %collective-permute-start.30 = (bf16[8,2,64,256]{3,2,1,0:T(8,128)(2,1)}, bf16[8,2,64,256]{3,2,1,0:T(8,128)(2,1)S(1)}, u32[]{:S(2)}, u32[]{:S(2)}) collective-permute-start(bf16[8,2,64,256]{3,2,1,0:T(8,128)(2,1)} %get-tuple-element.167), channel_id=1, source_target_pairs={{0,16},{2,18},{4,20},{6,22},{8,24},{10,26},{12,28},{14,30},{16,0},... | collective-permute-start | bytes 1572872 | tf_op jit(solution)/shard_map/ppermute | solution.py:28
  351.4 41.3 %collective-permute-start.37 = (bf16[8,2,64,256]{3,2,1,0:T(8,128)(2,1)}, bf16[8,2,64,256]{3,2,1,0:T(8,128)(2,1)}, u32[]{:S(2)}, u32[]{:S(2)}) collective-permute-start(bf16[8,2,64,256]{3,2,1,0:T(8,128)(2,1)} %get-tuple-element.184), channel_id=1, source_target_pairs={{0,8},{2,10},{4,12},{6,14},{8,0},{10,2},{12,4},{14,6},{16,24},{18,... | collective-permute-start | bytes 1572872 | tf_op jit(solution)/shard_map/ppermute | solution.py:28
  363.0 39.3 %collective-permute-start.36 = (bf16[8,2,64,256]{3,2,1,0:T(8,128)(2,1)}, bf16[8,2,64,256]{3,2,1,0:T(8,128)(2,1)S(1)}, u32[]{:S(2)}, u32[]{:S(2)}) collective-permute-start(bf16[8,2,64,256]{3,2,1,0:T(8,128)(2,1)} %get-tuple-element.182), channel_id=1, source_target_pairs={{0,24},{2,26},{4,28},{6,30},{8,16},{10,18},{12,20},{14,22},{16,8},... | collective-permute-start | bytes 1572872 | tf_op jit(solution)/shard_map/ppermute | solution.py:28
  395.0 29.5 %collective-permute-start.41 = (bf16[8,2,64,256]{3,2,1,0:T(8,128)(2,1)}, bf16[8,2,64,256]{3,2,1,0:T(8,128)(2,1)S(1)}, u32[]{:S(2)}, u32[]{:S(2)}) collective-permute-start(bf16[8,2,64,256]{3,2,1,0:T(8,128)(2,1)} %get-tuple-element.190), channel_id=1, source_target_pairs={{0,16},{2,18},{4,20},{6,22},{8,24},{10,26},{12,28},{14,30},{16,0},... | collective-permute-start | bytes 1572872 | tf_op jit(solution)/shard_map/ppermute | solution.py:28
  408.3 38.1 %collective-permute-start.43 = (bf16[8,2,64,256]{3,2,1,0:T(8,128)(2,1)}, bf16[8,2,64,256]{3,2,1,0:T(8,128)(2,1)S(1)}, u32[]{:S(2)}, u32[]{:S(2)}) collective-permute-start(bf16[8,2,64,256]{3,2,1,0:T(8,128)(2,1)} %get-tuple-element.191), channel_id=1, source_target_pairs={{0,8},{2,10},{4,12},{6,14},{8,0},{10,2},{12,4},{14,6},{16,24},{18,... | collective-permute-start | bytes 1572872 | tf_op jit(solution)/shard_map/ppermute | solution.py:28
  416.0 33.2 %collective-permute-start.45 = (bf16[8,2,64,256]{3,2,1,0:T(8,128)(2,1)}, bf16[8,2,64,256]{3,2,1,0:T(8,128)(2,1)S(1)}, u32[]{:S(2)}, u32[]{:S(2)}) collective-permute-start(bf16[8,2,64,256]{3,2,1,0:T(8,128)(2,1)} %get-tuple-element.192), channel_id=1, source_target_pairs={{0,24},{2,26},{4,28},{6,30},{8,16},{10,18},{12,20},{14,22},{16,8},... | collective-permute-start | bytes 1572872 | tf_op jit(solution)/shard_map/ppermute | solution.py:28
  (74 other events, 976.0 us)
